TPU v7x, 128 devices: a whole 4x4x4 slice. The times are simulated.
128 devices in a mesh: leaf: 8 (over z, core), sub: 16 (over x, y).
Axes of the slice: x: 4, y: 4, z: 4, core: 2. Of those that a mesh axis runs over, the one named last changes fastest.
Arguments:
- leaf_matrix: float32 [128, 512, 512], P(('leaf', 'sub')), may hold values from 0 to 4, as said below
- leaf_source: float32 [128, 512], P(('leaf', 'sub')), may hold values from -6 to 6
- observe: float32 [128, 512], P(('leaf', 'sub')), may hold values from -6 to 6
- zone_ids: int32 [128, 512], P(('leaf', 'sub')), may hold values from 0 to 16383
- log_perm: float32 [16384], P(('leaf', 'sub')), may hold values from -1 to 1
- block_map: int32 [254, 4], replicated, may hold values from 0 to 6, as said below
Outputs:
- leaf_solution: float32 [128, 512], P(('leaf', 'sub'))
- gradient: float32 [16384], P(('leaf', 'sub'))
Inputs may be any that keep to these rules, and one draw needn't show every extreme that they name: `block_map`: rows 2q and 2q + 1 (sibling nodes) each hold 4 distinct blocks; together they name every value from 0 to 6, sharing exactly one. Each leaf_matrix[d] is symmetric and positive definite.
All inputs are finite; a program needn't handle non-finite values.
Results may differ from a plain program's by a relative error of at most 0.0003.
Values sent between devices are 32-bit elements; how exact they have to be, the bound alone decides.
No kernel may reach another device: no remote copies, remote signals or barrier semaphores. Data moves between devices by JAX's collectives and lax.ppermute only.
A program may use at most 128 MiB of HBM per device.

v0:
```python
import functools

import jax
import jax.numpy as jnp
from jax import lax
from jax.experimental import pallas as pl
from jax.experimental.pallas import tpu as pltpu
from jax.sharding import PartitionSpec as P

BW = 128
NB = 4
KEEP = NB - 1
FW = NB * BW
NEVER = 99
STRIDE = 16
VMEM_LIMIT = 48 * 1024 * 1024


def split(x):
    high = x.astype(jnp.bfloat16)
    return high, (x - high.astype(jnp.float32)).astype(jnp.bfloat16)


def dot_split(a, b):
    one = functools.partial(jnp.dot, preferred_element_type=jnp.float32)
    both = one(jnp.concatenate([a[0], a[1]], 1), jnp.concatenate([b[0], b[0]], 0))
    return both + one(a[0], b[1])


def dot_split_left(a, b):
    one = functools.partial(
        lax.dot_general, dimension_numbers=(((0,), (0,)), ((), ())), preferred_element_type=jnp.float32
    )
    both = one(jnp.concatenate([a[0], a[1]], 0), jnp.concatenate([b[0], b[0]], 0))
    return both + one(a[0], b[1])


def dot_split_right(a, b):
    one = functools.partial(
        lax.dot_general, dimension_numbers=(((1,), (1,)), ((), ())), preferred_element_type=jnp.float32
    )
    both = one(jnp.concatenate([a[0], a[1]], 1), jnp.concatenate([b[0], b[0]], 1))
    return both + one(a[0], b[1])


def lanes(x, c):
    return jnp.broadcast_to(x[:, c : c + 1], (8, BW))


def rows(x, j):
    return jnp.broadcast_to(x[j : j + 1, :], (8, BW))


def pivots(row, cols, sub):
    for j in range(0, 8, 2):
        left, right = cols[j], cols[j + 1]
        a, b, c = rows(left, j), rows(left, j + 1), rows(right, j + 1)
        scale = 1.0 / (a * c - b * b)
        first, second = sub == j, sub == j + 1

        def update(v):
            v0, v1 = rows(v, j), rows(v, j + 1)
            u0 = c * v0 - b * v1
            u1 = a * v1 - b * v0
            t = left * u0 + right * u1
            return jnp.where(first, u0 * scale, jnp.where(second, u1 * scale, v - t * scale))

        row = update(row)
        for m in range(j + 2, 8):
            cols[m] = update(cols[m])
    return row


def invert(slabs):
    lane = lax.broadcasted_iota(jnp.int32, (8, BW), 1)
    sub = lax.broadcasted_iota(jnp.int32, (8, BW), 0)
    slabs = list(slabs)
    count = len(slabs)
    half = count // 2
    for panel in (range(half), range(half, count)):
        for k in panel:
            cols = [lanes(slabs[k], 8 * k + j) for j in range(8)]
            inside = (lane >= 8 * k) & (lane < 8 * k + 8)
            row = jnp.where(lane == sub + 8 * k, 1.0, jnp.where(inside, 0.0, slabs[k]))
            row = pivots(row, cols, sub)
            w = [rows(row, j) for j in range(8)]
            for r in [r for r in panel if r > k] + [r for r in panel if r < k]:
                t0 = jnp.where(inside, 0.0, slabs[r]) - lanes(slabs[r], 8 * k) * w[0]
                t1 = lanes(slabs[r], 8 * k + 1) * w[1]
                for j in range(2, 8, 2):
                    t0 = t0 - lanes(slabs[r], 8 * k + j) * w[j]
                    t1 = t1 + lanes(slabs[r], 8 * k + j + 1) * w[j + 1]
                slabs[r] = t0 - t1
            slabs[k] = row
        start, stop = 8 * panel[0], 8 * panel[-1] + 8
        inside = (lane >= start) & (lane < stop)
        rest = [r for r in range(count) if r not in panel]
        g = jnp.concatenate([slabs[r][:, start:stop] for r in rest], 0)
        change = dot_split(split(g), split(jnp.concatenate([slabs[r] for r in panel], 0)))
        for n, r in enumerate(rest):
            slabs[r] = jnp.where(inside, 0.0, slabs[r]) - change[8 * n : 8 * n + 8]
    return slabs


def span(block):
    return pl.ds(pl.multiple_of(block * BW, BW), BW)


def invert_ref(load, store):
    out = invert([load(8 * r) for r in range(BW // 8)])
    for r in range(BW // 8):
        store[8 * r : 8 * r + 8, :] = out[r]


def sweep(front, inverse, wide, block):
    at = pl.multiple_of(block * BW, BW)
    invert_ref(lambda r: front[pl.ds(at + r, 8), pl.ds(at, BW)], inverse)
    wide[...] = dot_split(split(inverse[...]), split(front[pl.ds(at, BW), :]))
    wide[:, pl.ds(at, BW)] = inverse[...]
    w = split(wide[...])
    for start, size in [(i * BW, BW) for i in range(NB)] + [(FW, 8)]:
        g = split(front[start : start + size, pl.ds(at, BW)])
        front[start : start + size, pl.ds(at, BW)] = jnp.zeros((size, BW), jnp.float32)
        front[start : start + size, :] -= dot_split(g, w)


def active(levels, level):
    return min(NB, levels - level)


def pairs(count):
    return [(a, b) for a in range(count) for b in range(a, count)]


def parts(count):
    return 1 if count * (count + 1) // 2 % 2 else 2


def part_rows(count):
    return len(pairs(count)) // parts(count) * BW + -(-count // parts(count)) * 8


def block_row(count, p):
    each = len(pairs(count)) // parts(count)
    return p // each * part_rows(count) + p % each * BW


def rhs_row(count, a):
    each = -(-count // parts(count))
    return a // each * part_rows(count) + len(pairs(count)) // parts(count) * BW + a % each * 8


def write_pack(front, pack, count, core, at, rhs, valid):
    size = part_rows(count)
    whole = pack.shape[0] == parts(count) * size

    def put(start, height, source, ok):
        part = start // size
        to = start if whole else start % size
        ok = ok if whole else ok & (core == part)

        @pl.when(ok)
        def _():
            pack[to : to + height, :] = source()

    for p, (a, b) in enumerate(pairs(count)):
        put(block_row(count, p), BW, lambda a=a, b=b: front[at(a), at(b)], valid(a) & valid(b))
    for a in range(count):
        put(rhs_row(count, a), 8, lambda a=a: front[rhs : rhs + 8, at(a)], valid(a))


def plan_kernel(levels, tree_ref, map_ref, plan, when, position):
    tree = tree_ref[0]
    for i in range(NB):
        when[levels * NB + i] = NEVER
        position[levels * NB + i] = -1
    for level in reversed(range(levels)):
        nodes, node = (1 << levels) >> level, tree >> level
        mine, yours = (
            [map_ref[(nodes + n - 2) * NB + i] for i in range(NB)] for n in (node, node ^ 1)
        )
        dropped = active(levels, level + 1)
        for child, other, base in ((mine, yours, 0), (yours, mine, 4)):
            after, spot, place = [], [], []
            for m in child:
                both = functools.reduce(jnp.logical_or, [m == o for o in other])
                above = (level + 1) * NB + jnp.maximum(m - KEEP, 0)
                later = jnp.where(m >= KEEP, when[above], NEVER)
                after.append(jnp.where(both, level, later))
                place.append(jnp.where(later < NEVER, position[above], jnp.where(both, dropped, -1)))
            for i in range(NB):
                ahead = functools.reduce(jnp.add, [jnp.where(after[k] < after[i], 1, 0) for k in range(NB) if k != i])
                spot.append(jnp.where(after[i] < NEVER, ahead, -1))
            for a in range(NB):
                slot, order = jnp.int32(-1), jnp.int32(-1)
                for i in range(NB):
                    slot = jnp.where(spot[i] == a, place[i], slot)
                    order = jnp.where(spot[i] == a, i, order)
                plan[level * STRIDE + base + a] = slot
                if level == 0 and base == 0:
                    plan[levels * STRIDE + a] = order
            if base == 0:
                for i in range(NB):
                    when[level * NB + i] = after[i]
                    position[level * NB + i] = spot[i]
                    if level == 0:
                        plan[levels * STRIDE + 4 + i] = spot[i]
        plan[level * STRIDE + 8] = jnp.where(plan[level * STRIDE] == dropped, 1, 0)


def leaf_kernel(levels, plan, leaf, source, observe, perm, front, pack, inverse, wide):
    front[0:FW, :] = leaf[...]
    eye = lax.broadcasted_iota(jnp.int32, (BW, BW), 0) == lax.broadcasted_iota(jnp.int32, (BW, BW), 1)
    for i in range(NB):
        at = slice(i * BW, i * BW + BW)
        front[at, at] += jnp.where(eye, jnp.broadcast_to(perm[:, at], (BW, BW)), 0.0)
    which = lax.broadcasted_iota(jnp.int32, (8, FW), 0)
    front[FW : FW + 8, :] = jnp.where(
        which == 0,
        jnp.broadcast_to(source[...], (8, FW)),
        jnp.where(which == 1, jnp.broadcast_to(observe[...], (8, FW)), 0.0),
    )
    order = [plan[levels * STRIDE + a] for a in range(NB)]

    def step(i, carry):
        @pl.when(plan[levels * STRIDE + 4 + i] < 0)
        def _():
            sweep(front, inverse, wide, i)

        return carry

    lax.fori_loop(0, NB, step, 0)
    count = active(levels, 0)
    write_pack(
        front, pack, count, 0, lambda a: span(jnp.maximum(order[a], 0)), FW, lambda a: order[a] >= 0
    )


def merge_kernel(levels, level, core_ref, plan, own, *rest):
    below, count = active(levels, level), active(levels, level + 1)
    core = core_ref[0]
    base = level * STRIDE
    if level > 0 and parts(below) == 2:
        same, swapped, *rest, theirs = rest
        size = part_rows(below)
        theirs[pl.ds(pl.multiple_of(core * size, 8), size), :] = same[...]
        theirs[pl.ds(pl.multiple_of((1 - core) * size, 8), size), :] = swapped[...]
    else:
        theirs, *rest = rest
    if count:
        coupling, reduced, front, pack, diagonal, inverse, coupled = rest
        front[...] = jnp.zeros(front.shape, jnp.float32)
        coupled[...] = jnp.zeros(coupled.shape, jnp.float32)
    else:
        reduced, diagonal, inverse = rest
    mine = [plan[base + a] for a in range(below)]
    yours = [plan[base + 4 + a] for a in range(below)]
    eliminated = plan[base + 8] == 1
    kept = plan[base + 8] == 0
    rhs = count * BW
    if level == 0:
        order = [jnp.maximum(plan[levels * STRIDE + a], 0) for a in range(below)]
        at, own_rhs = lambda a: span(order[a]), FW
    else:
        at, own_rhs = lambda a: slice(a * BW, a * BW + BW), below * BW
    their_rows = {p: block_row(below, n) for n, p in enumerate(pairs(below))}
    their_block = lambda a, b: theirs[their_rows[a, b] : their_rows[a, b] + BW, :]
    their_rhs = lambda a: theirs[rhs_row(below, a) : rhs_row(below, a) + 8, :]
    diagonal[...] = own[at(0), at(0)] + their_block(0, 0)
    right = own[own_rhs : own_rhs + 8, at(0)] + their_rhs(0)
    reduced[...] = right

    def put(ok, a, b, value):
        @pl.when(ok)
        def _():
            front[span(a), span(b)] = value()

    def put_rhs(ok, a, value):
        @pl.when(ok)
        def _():
            front[rhs : rhs + 8, span(a)] = value()

    if count:
        put(kept, mine[0], mine[0], lambda: diagonal[...])
        put_rhs(kept, mine[0], lambda: reduced[...])
        for a in range(1, below):
            for slots, block, across, vector in (
                (mine, lambda a, b: own[at(a), at(b)], lambda a, b: own[at(b), at(a)], lambda a: own[own_rhs : own_rhs + 8, at(a)]),
                (yours, their_block, lambda a, b: their_block(a, b).T, their_rhs),
            ):
                there = slots[a] >= 0

                @pl.when(there & eliminated)
                def _():
                    coupled[:, span(slots[a])] = block(0, a)

                put(there & kept, slots[0], slots[a], lambda: block(0, a))
                put(there & kept, slots[a], slots[0], lambda: across(0, a))
                put_rhs(there, slots[a], lambda: vector(a))
                for b in range(a, below):
                    both = there & (slots[b] >= 0)
                    put(both, slots[a], slots[b], lambda: block(a, b))
                    if a != b:
                        put(both, slots[b], slots[a], lambda: across(a, b))

    @pl.when(eliminated)
    def _():
        invert_ref(lambda r: diagonal[r : r + 8, :], inverse)
        d, r = split(inverse[...]), split(reduced[...])
        if count:
            c = split(coupled[...])
            w = dot_split(d, c)
            coupling[...] = w
            w = split(w)
            front[0:rhs, :] -= dot_split_left(c, w)
            front[rhs : rhs + 8, :] -= dot_split(r, w)
        reduced[...] = dot_split(r, d)

    if count:

        @pl.when(kept)
        def _():
            coupling[...] = jnp.zeros(coupling.shape, jnp.float32)

        write_pack(
            front, pack, count, core, lambda a: slice(a * BW, a * BW + BW), rhs, lambda a: plan[0] == plan[0]
        )


def pick(blocks, slot):
    out = jnp.zeros((8, BW), jnp.float32)
    for n, block in enumerate(blocks):
        out = jnp.where(slot == n, block, out)
    return out


def recover_kernel(levels, plan, *refs):
    couplings, reduced = refs[: levels - 1], refs[levels - 1 : 2 * levels - 1]
    leaf, out = refs[2 * levels - 1 :]
    solved = [reduced[levels - 1][...]]
    for level in reversed(range(1, levels)):
        kept = [pick(solved, plan[level * STRIDE + a]) for a in range(active(levels, level))]
        z = split(jnp.concatenate(kept, 1))
        solved = kept + [reduced[level - 1][...] - dot_split_right(z, split(couplings[level - 1][...]))]
    spots = [plan[levels * STRIDE + 4 + i] for i in range(NB)]
    kept = [pick(solved, jnp.where(spot >= 0, plan[jnp.maximum(spot, 0)], -1)) for spot in spots]
    new = dot_split(split(jnp.concatenate(kept, 1)), split(leaf[0:FW, :])) - leaf[FW : FW + 8, :]
    for i in range(NB):
        at = slice(i * BW, i * BW + BW)
        out[:, at] = jnp.where(spots[i] >= 0, kept[i], new[:, at])


SCALARS = pl.BlockSpec(memory_space=pltpu.SMEM)
WHOLE = pl.BlockSpec(memory_space=pltpu.VMEM)
PARAMS = pltpu.CompilerParams(vmem_limit_bytes=VMEM_LIMIT)


def f32(*shape):
    return jax.ShapeDtypeStruct(shape, jnp.float32)


def vmem(*shape):
    return pltpu.VMEM(shape, jnp.float32)


def make_plan(levels, tree, maps):
    return pl.pallas_call(
        functools.partial(plan_kernel, levels),
        out_shape=jax.ShapeDtypeStruct(((levels + 1) * STRIDE,), jnp.int32),
        in_specs=[SCALARS, SCALARS],
        out_specs=SCALARS,
        scratch_shapes=[pltpu.SMEM(((levels + 1) * NB,), jnp.int32)] * 2,
        name="make_plan",
    )(tree, maps)


def leaf_front(levels, plan, leaf, source, observe, perm):
    count = active(levels, 0)
    return pl.pallas_call(
        functools.partial(leaf_kernel, levels),
        out_shape=(f32(FW + 8, FW), f32(parts(count) * part_rows(count), BW)),
        in_specs=[SCALARS] + [WHOLE] * 4,
        out_specs=(WHOLE, WHOLE),
        scratch_shapes=[vmem(BW, BW), vmem(BW, FW)],
        compiler_params=PARAMS,
        name="leaf_front",
    )(plan, leaf, source, observe, perm)


def merge(levels, level, core, plan, own, theirs):
    below, count = active(levels, level), active(levels, level + 1)
    n = count * BW
    out, work = (f32(8, BW),), [vmem(BW, BW), vmem(BW, BW)]
    if count:
        out = (f32(BW, n),) + out + (f32(n + 8, n), f32(part_rows(count), BW))
        work += [vmem(BW, n)]
    if len(theirs) == 2:
        work += [vmem(2 * part_rows(below), BW)]
    return pl.pallas_call(
        functools.partial(merge_kernel, levels, level),
        out_shape=out,
        in_specs=[SCALARS, SCALARS, WHOLE] + [WHOLE] * len(theirs),
        out_specs=(WHOLE,) * len(out),
        scratch_shapes=work,
        compiler_params=PARAMS,
        name=f"merge_{level}",
    )(core, plan, own, *theirs)


def recover(levels, plan, couplings, reduced, leaf):
    return pl.pallas_call(
        functools.partial(recover_kernel, levels),
        out_shape=f32(8, FW),
        in_specs=[SCALARS] + [WHOLE] * (2 * levels),
        out_specs=WHOLE,
        compiler_params=PARAMS,
        name="recover",
    )(plan, *couplings, *reduced, leaf)


def partner(block, axis, bit):
    count = lax.axis_size(axis)
    return lax.ppermute(block, axis, [(k, k ^ (1 << bit)) for k in range(count)])


def shards(leaf_matrix, leaf_source, observe, zone_ids, log_perm, block_map):
    leaf_count = lax.axis_size("leaf")
    devices = leaf_count * lax.axis_size("sub")
    leaf_bits = leaf_count.bit_length() - 1
    levels = devices.bit_length() - 1
    tree = (lax.axis_index("leaf") + leaf_count * lax.axis_index("sub")).astype(jnp.int32)[None]
    core = tree & 1
    plan = make_plan(levels, tree, block_map.reshape(-1))
    zones = jnp.broadcast_to(log_perm[None], (devices, log_perm.shape[0]))
    all_zones = lax.all_to_all(zones, ("leaf", "sub"), 0, 0, tiled=True).reshape(-1)
    cells = zone_ids[0]
    perm = jnp.exp(all_zones[cells])
    leaf, pack = leaf_front(levels, plan, leaf_matrix[0], leaf_source, observe, perm[None])
    front, couplings, reduced = leaf, [], []
    for level in range(levels):
        axis, bit = ("leaf", level) if level < leaf_bits else ("sub", level - leaf_bits)
        theirs = (partner(pack, axis, bit),)
        if level > 0 and parts(active(levels, level)) == 2:
            theirs += (partner(theirs[0], "leaf", 0),)
        *more, front, pack = merge(levels, level, core, plan, front, theirs) + ((None, None) if level == levels - 1 else ())
        couplings += more[:-1]
        reduced += more[-1:]
    solution = recover(levels, plan, couplings, reduced, leaf)
    terms = -perm * solution[0] * solution[1]
    partial = jax.ops.segment_sum(terms, cells, num_segments=all_zones.shape[0])
    shares = lax.all_to_all(partial.reshape(devices, -1), ("leaf", "sub"), 0, 0, tiled=True)
    return solution[0][None, :], shares.sum(0)


def solution(mesh):
    split_all = ("leaf", "sub")
    in_specs = (P(split_all, None, None), P(split_all, None), P(split_all, None), P(split_all, None), P(split_all), P())
    out_specs = (P(split_all, None), P(split_all))
    return jax.shard_map(shards, mesh=mesh, in_specs=in_specs, out_specs=out_specs, check_vma=False)
```

profile of v0, /device:TPU:1, one launch (start us, length us, event | category | flops | bytes accessed | tf_op | source)
XLA Modules:
  0.0 162.7 jit_solution(5301486461886585813)
XLA Ops:
  0.6 1.3 broadcast_in_dim.7
  1.9 11.5 %all-to-all-start = ((f32[128,1,128]{2,1,0:T(1,128)}), f32[128,1,128]{2,1,0:T(1,128)S(1)}, u32[]{:S(2)}, u32[]{:S(2)}) async-start(f32[128,1,128]{2,1,0:T(1,128)} %broadcast_in_dim.7), calls=%async_computation | async-start | bytes 131072 | tf_op jit(solution)/shard_map/all_to_all | solution.py:435
  13.4 0.7 compare_select_fusion
  14.1 0.8 copy.10
  14.9 0.7 reshape.57.map_ref
  15.7 2.1 %make_plan.1.plan = s32[128]{0:T(128)} custom-call(s32[1]{0:T(128)} %bitcast.tree_ref, s32[1016]{0:T(1024)} %reshape.57.map_ref), custom_call_target="tpu_custom_call" | custom-call | tf_op jit(solution)/shard_map/make_plan/pallas_call | solution.py:367
  17.8 0.0 copy-start.1
  17.8 5.2 %all-to-all-done = f32[128,1,128]{2,1,0:T(1,128)S(1)} async-done(((f32[128,1,128]{2,1,0:T(1,128)}), f32[128,1,128]{2,1,0:T(1,128)S(1)}, u32[]{:S(2)}, u32[]{:S(2)}) %all-to-all-start) | async-done | bytes 65568 | tf_op jit(solution)/shard_map/all_to_all | solution.py:435
  23.0 3.1 %gather_fusion = f32[512]{0:T(512)S(1)} fusion(f32[16384]{0:T(1024)S(1)} %bitcast.14, s32[1024]{0:T(1024)S(1)} %pad_clamp_fusion), kind=kCustom, calls=%fused_computation | custom fusion | bytes 6144 | tf_op jit(solution)/shard_map/gather | solution.py:437
  26.2 0.0 copy-done
  26.2 0.0 copy-done.2
  26.2 0.0 copy-done.3
  26.2 0.0 copy-done.1
  26.2 17.1 %leaf_front.1 = (f32[520,512]{1,0:T(8,128)S(1)}, f32[1312,128]{1,0:T(8,128)S(1)}) custom-call(s32[128]{0:T(128)S(1)} %copy-done.1, f32[512,512]{1,0:T(8,128)S(1)} %bitcast.12, f32[1,512]{1,0:T(1,128)S(1)} %copy-done.2, f32[1,512]{1,0:T(1,128)S(1)} %copy-done.3, f32[1,512]{1,0:T(1,128)S(1)} %bitcast.13), custom_call_target="tpu_custom_call" | custom-call | tf_op jit(solution)/shard_map/leaf_front/pallas_call | solution.py:379
  43.3 0.1 collective-permute-start
  43.4 2.1 %collective-permute-done.rest_0_ = f32[1312,128]{1,0:T(8,128)S(1)} collective-permute-done((f32[1312,128]{1,0:T(8,128)S(1)}, f32[1312,128]{1,0:T(8,128)S(1)}, u32[]{:S(2)}, u32[]{:S(2)}) %collective-permute-start) | collective-permute-done | bytes 671776 | tf_op jit(solution)/shard_map/ppermute | solution.py:423
  45.5 5.7 %merge_0.1 = (f32[128,512]{1,0:T(8,128)S(1)}, f32[8,128]{1,0:T(8,128)S(1)}, f32[520,512]{1,0:T(8,128)S(1)}, f32[656,128]{1,0:T(8,128)S(1)}) custom-call(s32[1]{0:T(128)S(6)} %and.5.core_ref, s32[128]{0:T(128)S(1)} %copy-done.1, f32[520,512]{1,0:T(8,128)S(1)} %get-tuple-element.28.own.refs_13_, f32[1312,128]{1,0:T(8,128)S(1)} %collective-permute-done.rest_0_), custom_call_target="tpu_custom_call" | custom-call | tf_op jit(solution)/shard_map/merge_0/pallas_call | solution.py:399
  51.2 0.1 collective-permute-start.1
  51.3 9.3 %collective-permute-done.1.rest_0_ = f32[656,128]{1,0:T(8,128)S(1)} collective-permute-done((f32[656,128]{1,0:T(8,128)S(1)}, f32[656,128]{1,0:T(8,128)S(1)}, u32[]{:S(2)}, u32[]{:S(2)}) %collective-permute-start.1) | collective-permute-done | bytes 335904 | tf_op jit(solution)/shard_map/ppermute | solution.py:423
  60.6 1.0 collective-permute-start.2
  61.6 1.3 collective-permute-done.2.rest_1_
  62.9 6.0 %merge_1.1 = (f32[128,512]{1,0:T(8,128)S(1)}, f32[8,128]{1,0:T(8,128)S(1)}, f32[520,512]{1,0:T(8,128)S(1)}, f32[656,128]{1,0:T(8,128)S(1)}) custom-call(s32[1]{0:T(128)S(6)} %and.5.core_ref, s32[128]{0:T(128)S(1)} %copy-done.1, f32[520,512]{1,0:T(8,128)S(1)} %get-tuple-element.31.own, f32[656,128]{1,0:T(8,128)S(1)} %collective-permute-done.1.rest_0_, ...), custom_call_target="tpu_custom_call" | custom-call | tf_op jit(solution)/shard_map/merge_1/pallas_call | solution.py:399
  68.9 1.3 collective-permute-start.3
  70.2 9.4 %collective-permute-done.3.rest_0_ = f32[656,128]{1,0:T(8,128)S(1)} collective-permute-done((f32[656,128]{1,0:T(8,128)S(1)}, f32[656,128]{1,0:T(8,128)S(1)}, u32[]{:S(2)}, u32[]{:S(2)}) %collective-permute-start.3) | collective-permute-done | bytes 335904 | tf_op jit(solution)/shard_map/ppermute | solution.py:423
  79.6 1.2 collective-permute-start.4
  80.8 1.3 collective-permute-done.4.rest_1_
  82.0 5.8 %merge_2.1 = (f32[128,512]{1,0:T(8,128)S(1)}, f32[8,128]{1,0:T(8,128)S(1)}, f32[520,512]{1,0:T(8,128)S(1)}, f32[656,128]{1,0:T(8,128)S(1)}) custom-call(s32[1]{0:T(128)S(6)} %and.5.core_ref, s32[128]{0:T(128)S(1)} %copy-done.1, f32[520,512]{1,0:T(8,128)S(1)} %get-tuple-element.34.own, f32[656,128]{1,0:T(8,128)S(1)} %collective-permute-done.3.rest_0_, ...), custom_call_target="tpu_custom_call" | custom-call | tf_op jit(solution)/shard_map/merge_2/pallas_call | solution.py:399
  87.8 0.1 collective-permute-start.5
  87.9 9.1 %collective-permute-done.5.rest_0_ = f32[656,128]{1,0:T(8,128)S(1)} collective-permute-done((f32[656,128]{1,0:T(8,128)S(1)}, f32[656,128]{1,0:T(8,128)S(1)}, u32[]{:S(2)}, u32[]{:S(2)}) %collective-permute-start.5) | collective-permute-done | bytes 335904 | tf_op jit(solution)/shard_map/ppermute | solution.py:423
  97.0 1.2 collective-permute-start.6
  98.2 1.3 collective-permute-done.6.rest_1_
  99.5 5.6 %merge_3.1 = (f32[128,384]{1,0:T(8,128)S(1)}, f32[8,128]{1,0:T(8,128)S(1)}, f32[392,384]{1,0:T(8,128)S(1)}, f32[400,128]{1,0:T(8,128)S(1)}) custom-call(s32[1]{0:T(128)S(6)} %and.5.core_ref, s32[128]{0:T(128)S(1)} %copy-done.1, f32[520,512]{1,0:T(8,128)S(1)} %get-tuple-element.37.own, f32[656,128]{1,0:T(8,128)S(1)} %collective-permute-done.5.rest_0_, ...), custom_call_target="tpu_custom_call" | custom-call | tf_op jit(solution)/shard_map/merge_3/pallas_call | solution.py:399
  105.1 0.1 collective-permute-start.7
  105.1 7.8 %collective-permute-done.7.rest_0_ = f32[400,128]{1,0:T(8,128)S(1)} collective-permute-done((f32[400,128]{1,0:T(8,128)S(1)}, f32[400,128]{1,0:T(8,128)S(1)}, u32[]{:S(2)}, u32[]{:S(2)}) %collective-permute-start.7) | collective-permute-done | bytes 204832 | tf_op jit(solution)/shard_map/ppermute | solution.py:423
  112.9 1.2 collective-permute-start.8
  114.1 1.1 collective-permute-done.8.rest_1_
  115.2 5.3 %merge_4.1 = (f32[128,256]{1,0:T(8,128)S(1)}, f32[8,128]{1,0:T(8,128)S(1)}, f32[264,256]{1,0:T(8,128)S(1)}, f32[400,128]{1,0:T(8,128)S(1)}) custom-call(s32[1]{0:T(128)S(6)} %and.5.core_ref, s32[128]{0:T(128)S(1)} %copy-done.1, f32[392,384]{1,0:T(8,128)S(1)} %get-tuple-element.40.own, f32[400,128]{1,0:T(8,128)S(1)} %collective-permute-done.7.rest_0_, ...), custom_call_target="tpu_custom_call" | custom-call | tf_op jit(solution)/shard_map/merge_4/pallas_call | solution.py:399
  120.6 0.3 collective-permute-start.9
  120.8 6.1 %collective-permute-done.9.rest_0_ = f32[400,128]{1,0:T(8,128)S(1)} collective-permute-done((f32[400,128]{1,0:T(8,128)S(1)}, f32[400,128]{1,0:T(8,128)S(1)}, u32[]{:S(2)}, u32[]{:S(2)}) %collective-permute-start.9) | collective-permute-done | bytes 204832 | tf_op jit(solution)/shard_map/ppermute | solution.py:423
  126.9 5.2 %merge_5.1 = (f32[128,128]{1,0:T(8,128)S(1)}, f32[8,128]{1,0:T(8,128)S(1)}, f32[136,128]{1,0:T(8,128)S(1)}, f32[136,128]{1,0:T(8,128)S(1)}) custom-call(s32[1]{0:T(128)S(6)} %and.5.core_ref, s32[128]{0:T(128)S(1)} %copy-done.1, f32[264,256]{1,0:T(8,128)S(1)} %get-tuple-element.43.own, f32[400,128]{1,0:T(8,128)S(1)} %collective-permute-done.9.rest_0_), custom_call_target="tpu_custom_call" | custom-call | tf_op jit(solution)/shard_map/merge_5/pallas_call | solution.py:399
  132.1 0.1 collective-permute-start.10
  132.2 4.7 %collective-permute-done.10.rest_0_ = f32[136,128]{1,0:T(8,128)S(1)} collective-permute-done((f32[136,128]{1,0:T(8,128)S(1)}, f32[136,128]{1,0:T(8,128)S(1)}, u32[]{:S(2)}, u32[]{:S(2)}) %collective-permute-start.10) | collective-permute-done | bytes 69664 | tf_op jit(solution)/shard_map/ppermute | solution.py:423
  136.9 4.5 %merge_6.1.refs_12_ = f32[8,128]{1,0:T(8,128)S(1)} custom-call(s32[1]{0:T(128)S(6)} %and.5.core_ref, s32[128]{0:T(128)S(1)} %copy-done.1, f32[136,128]{1,0:T(8,128)S(1)} %get-tuple-element.52.own, f32[136,128]{1,0:T(8,128)S(1)} %collective-permute-done.10.rest_0_), custom_call_target="tpu_custom_call" | custom-call | tf_op jit(solution)/shard_map/merge_6/pallas_call | solution.py:399
  141.4 2.4 %recover.1 = f32[8,512]{1,0:T(8,128)S(1)} custom-call(s32[128]{0:T(128)S(1)} %copy-done.1, f32[128,512]{1,0:T(8,128)S(1)} %get-tuple-element.30.refs_0_, f32[128,512]{1,0:T(8,128)S(1)} %get-tuple-element.33.refs_1_, f32[128,512]{1,0:T(8,128)S(1)} %get-tuple-element.36.refs_2_, f32[128,384]{1,0:T(8,128)S(1)} %get-tuple-element.39.refs_3_, ...), custom_call_target="tpu_custom_call" | custom-call | tf_op jit(solution)/shard_map/recover/pallas_call | solution.py:411
  143.8 0.0 copy-start.4
  143.9 3.4 %scatter_custom_fusion = f32[16384]{0:T(1024)S(1)} fusion(s32[512]{0:T(512)} %bitcast.20, f32[512]{0:T(512)S(1)} %multiply_multiply_fusion, f32[]{:T(128)} %constant.19.clone.1), kind=kCustom, calls=%fused_computation.2 | custom fusion | flops 512 | bytes 66048 | tf_op jit(solution)/shard_map/scatter-add | solution.py:450
  147.3 14.8 %all_to_all.15 = f32[128,1,128]{2,1,0:T(1,128)S(1)} all-to-all(f32[128,1,128]{2,1,0:T(1,128)S(1)} %bitcast.16), channel_id=1, replica_groups=mesh['leaf'=8,'sub'=16] {'leaf','sub'}, dimensions={0} | all-to-all | bytes 131072 | tf_op jit(solution)/shard_map/all_to_all | solution.py:451
  162.1 0.5 reduce_sum.9
  (8 shorter events, 0.0 us)
Async XLA Ops:
  1.9 21.1 %all-to-all-start = ((f32[128,1,128]{2,1,0:T(1,128)}), f32[128,1,128]{2,1,0:T(1,128)S(1)}, u32[]{:S(2)}, u32[]{:S(2)}) async-start(f32[128,1,128]{2,1,0:T(1,128)} %broadcast_in_dim.7), calls=%async_computation | async-start | bytes 131072 | tf_op jit(solution)/shard_map/all_to_all | solution.py:435
  15.7 10.5 %copy-start = (f32[1,512,512]{2,1,0:T(8,128)S(1)}, f32[1,512,512]{2,1,0:T(8,128)}, u32[]{:S(2)}) copy-start(f32[1,512,512]{2,1,0:T(8,128)} %param.6) | copy-start | bytes 3145732
  15.7 10.5 %copy-start.2 = (f32[1,512]{1,0:T(1,128)S(1)}, f32[1,512]{1,0:T(1,128)}, u32[]{:S(2)}) copy-start(f32[1,512]{1,0:T(1,128)} %source.1) | copy-start | bytes 6148
  15.7 10.5 %copy-start.3 = (f32[1,512]{1,0:T(1,128)S(1)}, f32[1,512]{1,0:T(1,128)}, u32[]{:S(2)}) copy-start(f32[1,512]{1,0:T(1,128)} %observe.1) | copy-start | bytes 6148
  17.8 8.4 %copy-start.1 = (s32[128]{0:T(128)S(1)}, s32[128]{0:T(128)}, u32[]{:S(2)}) copy-start(s32[128]{0:T(128)} %make_plan.1.plan) | copy-start | bytes 1540
  43.3 2.2 %collective-permute-start = (f32[1312,128]{1,0:T(8,128)S(1)}, f32[1312,128]{1,0:T(8,128)S(1)}, u32[]{:S(2)}, u32[]{:S(2)}) collective-permute-start(f32[1312,128]{1,0:T(8,128)S(1)} %get-tuple-element.29), channel_id=1, source_target_pairs={{0,16},{16,0},{32,48},{48,32},{64,80},{80,64},{96,112},{112,96},{1... | collective-permute-start | bytes 2015240 | tf_op jit(solution)/shard_map/ppermute | solution.py:423
  51.2 9.4 %collective-permute-start.1 = (f32[656,128]{1,0:T(8,128)S(1)}, f32[656,128]{1,0:T(8,128)S(1)}, u32[]{:S(2)}, u32[]{:S(2)}) collective-permute-start(f32[656,128]{1,0:T(8,128)S(1)} %get-tuple-element.32), channel_id=1, source_target_pairs={{0,32},{16,48},{32,0},{48,16},{64,96},{80,112},{96,64},{112,80},{1... | collective-permute-start | bytes 1007624 | tf_op jit(solution)/shard_map/ppermute | solution.py:423
  60.6 2.2 %collective-permute-start.2 = (f32[656,128]{1,0:T(8,128)S(1)}, f32[656,128]{1,0:T(8,128)S(1)}, u32[]{:S(2)}, u32[]{:S(2)}) collective-permute-start(f32[656,128]{1,0:T(8,128)S(1)} %collective-permute-done.1.rest_0_), channel_id=1, source_target_pairs={{0,16},{16,0},{32,48},{48,32},{64,80},{80,64},{96,112},{112,96},{1... | collective-permute-start | bytes 1007624 | tf_op jit(solution)/shard_map/ppermute | solution.py:423
  68.9 10.7 %collective-permute-start.3 = (f32[656,128]{1,0:T(8,128)S(1)}, f32[656,128]{1,0:T(8,128)S(1)}, u32[]{:S(2)}, u32[]{:S(2)}) collective-permute-start(f32[656,128]{1,0:T(8,128)S(1)} %get-tuple-element.35), channel_id=1, source_target_pairs={{0,64},{16,80},{32,96},{48,112},{64,0},{80,16},{96,32},{112,48},{1... | collective-permute-start | bytes 1007624 | tf_op jit(solution)/shard_map/ppermute | solution.py:423
  79.6 2.5 %collective-permute-start.4 = (f32[656,128]{1,0:T(8,128)S(1)}, f32[656,128]{1,0:T(8,128)S(1)}, u32[]{:S(2)}, u32[]{:S(2)}) collective-permute-start(f32[656,128]{1,0:T(8,128)S(1)} %collective-permute-done.3.rest_0_), channel_id=1, source_target_pairs={{0,16},{16,0},{32,48},{48,32},{64,80},{80,64},{96,112},{112,96},{1... | collective-permute-start | bytes 1007624 | tf_op jit(solution)/shard_map/ppermute | solution.py:423
  87.8 9.2 %collective-permute-start.5 = (f32[656,128]{1,0:T(8,128)S(1)}, f32[656,128]{1,0:T(8,128)S(1)}, u32[]{:S(2)}, u32[]{:S(2)}) collective-permute-start(f32[656,128]{1,0:T(8,128)S(1)} %get-tuple-element.38), channel_id=1, source_target_pairs={{0,1},{1,0},{2,3},{3,2},{4,5},{5,4},{6,7},{7,6},{8,9},{9,8},{10,11... | collective-permute-start | bytes 1007624 | tf_op jit(solution)/shard_map/ppermute | solution.py:423
  97.0 2.5 %collective-permute-start.6 = (f32[656,128]{1,0:T(8,128)S(1)}, f32[656,128]{1,0:T(8,128)S(1)}, u32[]{:S(2)}, u32[]{:S(2)}) collective-permute-start(f32[656,128]{1,0:T(8,128)S(1)} %collective-permute-done.5.rest_0_), channel_id=1, source_target_pairs={{0,16},{16,0},{32,48},{48,32},{64,80},{80,64},{96,112},{112,96},{1... | collective-permute-start | bytes 1007624 | tf_op jit(solution)/shard_map/ppermute | solution.py:423
  105.1 7.9 %collective-permute-start.7 = (f32[400,128]{1,0:T(8,128)S(1)}, f32[400,128]{1,0:T(8,128)S(1)}, u32[]{:S(2)}, u32[]{:S(2)}) collective-permute-start(f32[400,128]{1,0:T(8,128)S(1)} %get-tuple-element.41), channel_id=1, source_target_pairs={{0,2},{1,3},{2,0},{3,1},{4,6},{5,7},{6,4},{7,5},{8,10},{9,11},{10,... | collective-permute-start | bytes 614408 | tf_op jit(solution)/shard_map/ppermute | solution.py:423
  112.9 2.3 %collective-permute-start.8 = (f32[400,128]{1,0:T(8,128)S(1)}, f32[400,128]{1,0:T(8,128)S(1)}, u32[]{:S(2)}, u32[]{:S(2)}) collective-permute-start(f32[400,128]{1,0:T(8,128)S(1)} %collective-permute-done.7.rest_0_), channel_id=1, source_target_pairs={{0,16},{16,0},{32,48},{48,32},{64,80},{80,64},{96,112},{112,96},{1... | collective-permute-start | bytes 614408 | tf_op jit(solution)/shard_map/ppermute | solution.py:423
  120.6 6.4 %collective-permute-start.9 = (f32[400,128]{1,0:T(8,128)S(1)}, f32[400,128]{1,0:T(8,128)S(1)}, u32[]{:S(2)}, u32[]{:S(2)}) collective-permute-start(f32[400,128]{1,0:T(8,128)S(1)} %get-tuple-element.44), channel_id=1, source_target_pairs={{0,4},{1,5},{2,6},{3,7},{4,0},{5,1},{6,2},{7,3},{8,12},{9,13},{10,... | collective-permute-start | bytes 614408 | tf_op jit(solution)/shard_map/ppermute | solution.py:423
  132.1 4.7 %collective-permute-start.10 = (f32[136,128]{1,0:T(8,128)S(1)}, f32[136,128]{1,0:T(8,128)S(1)}, u32[]{:S(2)}, u32[]{:S(2)}) collective-permute-start(f32[136,128]{1,0:T(8,128)S(1)} %get-tuple-element.53), channel_id=1, source_target_pairs={{0,8},{1,9},{2,10},{3,11},{4,12},{5,13},{6,14},{7,15},{8,0},{9,1},... | collective-permute-start | bytes 208904 | tf_op jit(solution)/shard_map/ppermute | solution.py:423
  143.8 18.8 %copy-start.4 = (f32[1,512]{1,0:T(1,128)}, f32[1,512]{1,0:T(1,128)S(1)}, u32[]{:S(2)}) copy-start(f32[1,512]{1,0:T(1,128)S(1)} %get-tuple-element.55) | copy-start | bytes 6148
where the time goes:
time: 164 us; the launch traced here: 163 us
  Pallas kernels  59.8 us (36%)
  waiting for transfers between devices  58.5 us (36%)
  starting transfers between devices  18.1 us (11%)
  blocking collectives  14.8 us (9%)
  local copies, waits for them, and re-layouts  6 us (4%)
  other arithmetic  4.66 us (3%)
    ppermute x11, waiting for transfers between devices, partner(): return lax.ppermute(block, axis, [(k, k ^ 1 << bit) for k in range(count)])  53.3 us
    pallas_call x7, Pallas kernels, merge(): pl.pallas_call(functools.partial(merge_kernel, levels, level), out_shape=...  38.2 us
    pallas_call x1, Pallas kernels, leaf_front(): pl.pallas_call(functools.partial(leaf_kernel, levels), out_shape=(f32(FW...  17.1 us
    all_to_all x1, blocking collectives, shards(): lax.all_to_all(partial.reshape(devices, -1), ('leaf', 'sub'), 0, 0, tiled...  14.8 us
    all_to_all x1, starting transfers between devices, shards(): lax.all_to_all(zones, ('leaf', 'sub'), 0, 0, tiled=True).reshape(-1)  11.5 us
    ppermute x11, starting transfers between devices, partner(): return lax.ppermute(block, axis, [(k, k ^ 1 << bit) for k in range(count)])  6.61 us
    all_to_all x1, waiting for transfers between devices, shards(): lax.all_to_all(zones, ('leaf', 'sub'), 0, 0, tiled=True).reshape(-1)  5.19 us
    scatter-add x1, other arithmetic, shards(): partial = jax.ops.segment_sum(terms, cells, num_segments=all_zones.shape[0])  3.42 us
  transfers between devices with their start and end apart: 12, of which 12 were waited for; matrix products, arithmetic and copies ran while one was open for 1% of the time, Pallas kernels for 1%

commit v1 on v0

--- a/solution.py
+++ b/solution.py
@@ -11,6 +11,7 @@
 NB = 4
 KEEP = NB - 1
 FW = NB * BW
+SLOTS = 64
 NEVER = 99
 STRIDE = 16
 VMEM_LIMIT = 48 * 1024 * 1024
@@ -51,38 +52,45 @@
     return jnp.broadcast_to(x[j : j + 1, :], (8, BW))
 
 
-def pivots(row, cols, sub):
+def pivots(row, cols, sub, buffer, slot):
+    def pair(v, j):
+        slot[0] = (slot[0] + 1) % SLOTS
+        at = 8 * slot[0]
+        buffer[at : at + 8, :] = v
+        return [jnp.broadcast_to(buffer[at + i : at + i + 1, :], (8, BW)) for i in (j, j + 1)]
+
     for j in range(0, 8, 2):
         left, right = cols[j], cols[j + 1]
-        a, b, c = rows(left, j), rows(left, j + 1), rows(right, j + 1)
+        spread = {m: pair(cols[m], j) for m in range(j, 8)}
+        a, b, c = spread[j][0], spread[j][1], spread[j + 1][1]
         scale = 1.0 / (a * c - b * b)
         first, second = sub == j, sub == j + 1
 
-        def update(v):
-            v0, v1 = rows(v, j), rows(v, j + 1)
+        def update(v, v0, v1):
             u0 = c * v0 - b * v1
             u1 = a * v1 - b * v0
             t = left * u0 + right * u1
             return jnp.where(first, u0 * scale, jnp.where(second, u1 * scale, v - t * scale))
 
-        row = update(row)
+        row = update(row, *pair(row, j))
         for m in range(j + 2, 8):
-            cols[m] = update(cols[m])
+            cols[m] = update(cols[m], *spread[m])
     return row
 
 
-def invert(slabs):
+def invert(slabs, buffer):
     lane = lax.broadcasted_iota(jnp.int32, (8, BW), 1)
     sub = lax.broadcasted_iota(jnp.int32, (8, BW), 0)
     slabs = list(slabs)
     count = len(slabs)
     half = count // 2
+    slot = [0]
     for panel in (range(half), range(half, count)):
         for k in panel:
             cols = [lanes(slabs[k], 8 * k + j) for j in range(8)]
             inside = (lane >= 8 * k) & (lane < 8 * k + 8)
             row = jnp.where(lane == sub + 8 * k, 1.0, jnp.where(inside, 0.0, slabs[k]))
-            row = pivots(row, cols, sub)
+            row = pivots(row, cols, sub, buffer, slot)
             w = [rows(row, j) for j in range(8)]
             for r in [r for r in panel if r > k] + [r for r in panel if r < k]:
                 t0 = jnp.where(inside, 0.0, slabs[r]) - lanes(slabs[r], 8 * k) * w[0]
@@ -106,15 +114,15 @@
     return pl.ds(pl.multiple_of(block * BW, BW), BW)
 
 
-def invert_ref(load, store):
-    out = invert([load(8 * r) for r in range(BW // 8)])
+def invert_ref(load, store, buffer):
+    out = invert([load(8 * r) for r in range(BW // 8)], buffer)
     for r in range(BW // 8):
         store[8 * r : 8 * r + 8, :] = out[r]
 
 
-def sweep(front, inverse, wide, block):
+def sweep(front, inverse, wide, buffer, block):
     at = pl.multiple_of(block * BW, BW)
-    invert_ref(lambda r: front[pl.ds(at + r, 8), pl.ds(at, BW)], inverse)
+    invert_ref(lambda r: front[pl.ds(at + r, 8), pl.ds(at, BW)], inverse, buffer)
     wide[...] = dot_split(split(inverse[...]), split(front[pl.ds(at, BW), :]))
     wide[:, pl.ds(at, BW)] = inverse[...]
     w = split(wide[...])
@@ -208,7 +216,7 @@
         plan[level * STRIDE + 8] = jnp.where(plan[level * STRIDE] == dropped, 1, 0)
 
 
-def leaf_kernel(levels, plan, leaf, source, observe, perm, front, pack, inverse, wide):
+def leaf_kernel(levels, plan, leaf, source, observe, perm, front, pack, inverse, wide, buffer):
     front[0:FW, :] = leaf[...]
     eye = lax.broadcasted_iota(jnp.int32, (BW, BW), 0) == lax.broadcasted_iota(jnp.int32, (BW, BW), 1)
     for i in range(NB):
@@ -225,7 +233,7 @@
     def step(i, carry):
         @pl.when(plan[levels * STRIDE + 4 + i] < 0)
         def _():
-            sweep(front, inverse, wide, i)
+            sweep(front, inverse, wide, buffer, i)
 
         return carry
 
@@ -236,7 +244,20 @@
     )
 
 
+def inverse_kernel(level, plan, own, theirs, inverse, buffer):
+    @pl.when(plan[level * STRIDE + 8] == 1)
+    def _():
+        inverse[...] = own[...] + theirs[...]
+        invert_ref(lambda r: inverse[r : r + 8, :], inverse, buffer)
+
+
+def early(levels, level):
+    return 0 < level < levels - 1
+
+
 def merge_kernel(levels, level, core_ref, plan, own, *rest):
+    if early(levels, level):
+        ahead, *rest = rest
     below, count = active(levels, level), active(levels, level + 1)
     core = core_ref[0]
     base = level * STRIDE
@@ -247,12 +268,16 @@
         theirs[pl.ds(pl.multiple_of((1 - core) * size, 8), size), :] = swapped[...]
     else:
         theirs, *rest = rest
+    if not early(levels, level):
+        *rest, ahead, buffer = rest
+    if early(levels, level + 1):
+        lead, *rest = rest
     if count:
-        coupling, reduced, front, pack, diagonal, inverse, coupled = rest
+        coupling, reduced, front, pack, diagonal, coupled = rest
         front[...] = jnp.zeros(front.shape, jnp.float32)
         coupled[...] = jnp.zeros(coupled.shape, jnp.float32)
     else:
-        reduced, diagonal, inverse = rest
+        reduced, diagonal = rest
     mine = [plan[base + a] for a in range(below)]
     yours = [plan[base + 4 + a] for a in range(below)]
     eliminated = plan[base + 8] == 1
@@ -305,8 +330,9 @@
 
     @pl.when(eliminated)
     def _():
-        invert_ref(lambda r: diagonal[r : r + 8, :], inverse)
-        d, r = split(inverse[...]), split(reduced[...])
+        if not early(levels, level):
+            invert_ref(lambda r: diagonal[r : r + 8, :], ahead, buffer)
+        d, r = split(ahead[...]), split(reduced[...])
         if count:
             c = split(coupled[...])
             w = dot_split(d, c)
@@ -325,6 +351,8 @@
         write_pack(
             front, pack, count, core, lambda a: slice(a * BW, a * BW + BW), rhs, lambda a: plan[0] == plan[0]
         )
+        if early(levels, level + 1):
+            lead[...] = front[0:BW, 0:BW]
 
 
 def pick(blocks, slot):
@@ -381,30 +409,47 @@
         out_shape=(f32(FW + 8, FW), f32(parts(count) * part_rows(count), BW)),
         in_specs=[SCALARS] + [WHOLE] * 4,
         out_specs=(WHOLE, WHOLE),
-        scratch_shapes=[vmem(BW, BW), vmem(BW, FW)],
+        scratch_shapes=[vmem(BW, BW), vmem(BW, FW), vmem(8 * SLOTS, BW)],
         compiler_params=PARAMS,
         name="leaf_front",
     )(plan, leaf, source, observe, perm)
 
 
-def merge(levels, level, core, plan, own, theirs):
+def shared_inverse(level, plan, own, theirs):
+    return pl.pallas_call(
+        functools.partial(inverse_kernel, level),
+        out_shape=f32(BW, BW),
+        in_specs=[SCALARS, WHOLE, WHOLE],
+        out_specs=WHOLE,
+        scratch_shapes=[vmem(8 * SLOTS, BW)],
+        compiler_params=PARAMS,
+        cost_estimate=pl.CostEstimate(flops=4 * BW**3, bytes_accessed=12 * BW * BW, transcendentals=0),
+        name=f"inverse_{level}",
+    )(plan, own, theirs)
+
+
+def merge(levels, level, core, plan, own, theirs, ahead):
     below, count = active(levels, level), active(levels, level + 1)
     n = count * BW
-    out, work = (f32(8, BW),), [vmem(BW, BW), vmem(BW, BW)]
+    out, work = (f32(8, BW),), [vmem(BW, BW)]
     if count:
         out = (f32(BW, n),) + out + (f32(n + 8, n), f32(part_rows(count), BW))
         work += [vmem(BW, n)]
+    if early(levels, level + 1):
+        out = (f32(BW, BW),) + out
+    if not early(levels, level):
+        work += [vmem(BW, BW), vmem(8 * SLOTS, BW)]
     if len(theirs) == 2:
         work += [vmem(2 * part_rows(below), BW)]
     return pl.pallas_call(
         functools.partial(merge_kernel, levels, level),
         out_shape=out,
-        in_specs=[SCALARS, SCALARS, WHOLE] + [WHOLE] * len(theirs),
+        in_specs=[SCALARS, SCALARS, WHOLE] + [WHOLE] * (len(theirs) + len(ahead)),
         out_specs=(WHOLE,) * len(out),
         scratch_shapes=work,
         compiler_params=PARAMS,
         name=f"merge_{level}",
-    )(core, plan, own, *theirs)
+    )(core, plan, own, *ahead, *theirs)
 
 
 def recover(levels, plan, couplings, reduced, leaf):
@@ -439,10 +484,19 @@
     front, couplings, reduced = leaf, [], []
     for level in range(levels):
         axis, bit = ("leaf", level) if level < leaf_bits else ("sub", level - leaf_bits)
+        ahead = ()
+        if early(levels, level):
+            ahead = (shared_inverse(level, plan, lead, partner(lead, axis, bit)),)
         theirs = (partner(pack, axis, bit),)
         if level > 0 and parts(active(levels, level)) == 2:
+            if ahead:
+                theirs, ahead = lax.optimization_barrier((theirs, ahead))
             theirs += (partner(theirs[0], "leaf", 0),)
-        *more, front, pack = merge(levels, level, core, plan, front, theirs) + ((None, None) if level == levels - 1 else ())
+        more = list(merge(levels, level, core, plan, front, theirs, ahead))
+        if early(levels, level + 1):
+            lead = more.pop(0)
+        if level < levels - 1:
+            *more, front, pack = more
         couplings += more[:-1]
         reduced += more[-1:]
     solution = recover(levels, plan, couplings, reduced, leaf)

time: 164 us -> 166 us (1.012)
  starting transfers between devices: 18.1 us -> 35.1 us
  Pallas kernels: 59.8 us -> 46.1 us
  blocking collectives: 14.8 us -> 20 us
  waiting for transfers between devices: 58.5 us -> 53.6 us
    pallas_call x7, Pallas kernels: 38.2 us -> 16.1 us  [merge(): pl.pallas_call(functools.partial(merge_kernel, levels, level), out_shape=...]
    ppermute x11 -> x16, starting transfers between devices: 6.61 us -> 23.6 us  [partner(): return lax.ppermute(block, axis, [(k, k ^ 1 << bit) for k in range(count)])]
    pallas_call x0 -> x5, Pallas kernels: none -> 14.3 us  [shared_inverse(): pl.pallas_call(functools.partial(inverse_kernel, level), out_shape=f32(BW...]
    pallas_call x1, Pallas kernels: 17.1 us -> 11.2 us  [leaf_front(): pl.pallas_call(functools.partial(leaf_kernel, levels), out_shape=(f32(FW...]
    all_to_all x1, blocking collectives: 14.8 us -> 20 us  [shards(): lax.all_to_all(partial.reshape(devices, -1), ('leaf', 'sub'), 0, 0, tiled...]
    ppermute x11 -> x16, waiting for transfers between devices: 53.3 us -> 48.4 us  [partner(): return lax.ppermute(block, axis, [(k, k ^ 1 << bit) for k in range(count)])]
  transfers between devices with their start and end apart: 12 -> 17, of which waited for: 12 -> 12; matrix products, arithmetic and copies ran while one was open for 1% -> 1% of each run, Pallas kernels for 1% -> 10%
where the time goes in v1:
time: 166 us
  waiting for transfers between devices  53.6 us (32%)
  Pallas kernels  46.1 us (28%)
  starting transfers between devices  35.1 us (21%)
  blocking collectives  20 us (12%)
  local copies, waits for them, and re-layouts  6.01 us (4%)
  other arithmetic  4.66 us (3%)
    ppermute x16, waiting for transfers between devices, partner(): return lax.ppermute(block, axis, [(k, k ^ 1 << bit) for k in range(count)])  48.4 us
    ppermute x16, starting transfers between devices, partner(): return lax.ppermute(block, axis, [(k, k ^ 1 << bit) for k in range(count)])  23.6 us
    all_to_all x1, blocking collectives, shards(): lax.all_to_all(partial.reshape(devices, -1), ('leaf', 'sub'), 0, 0, tiled...  20 us
    pallas_call x7, Pallas kernels, merge(): pl.pallas_call(functools.partial(merge_kernel, levels, level), out_shape=...  16.1 us
    pallas_call x5, Pallas kernels, shared_inverse(): pl.pallas_call(functools.partial(inverse_kernel, level), out_shape=f32(BW...  14.3 us
    all_to_all x1, starting transfers between devices, shards(): lax.all_to_all(zones, ('leaf', 'sub'), 0, 0, tiled=True).reshape(-1)  11.5 us
    pallas_call x1, Pallas kernels, leaf_front(): pl.pallas_call(functools.partial(leaf_kernel, levels), out_shape=(f32(FW...  11.2 us
    all_to_all x1, waiting for transfers between devices, shards(): lax.all_to_all(zones, ('leaf', 'sub'), 0, 0, tiled=True).reshape(-1)  5.19 us
  transfers between devices with their start and end apart: 17, of which 12 were waited for; matrix products, arithmetic and copies ran while one was open for 1% of the time, Pallas kernels for 10%

profile of v1, /device:TPU:1, one launch (start us, length us, event | category | flops | bytes accessed | tf_op | source)
XLA Modules:
  0.0 166.3 jit_solution(15547511180103075640)
XLA Ops:
  0.6 1.3 broadcast_in_dim.7
  1.9 11.5 %all-to-all-start = ((f32[128,1,128]{2,1,0:T(1,128)}), f32[128,1,128]{2,1,0:T(1,128)S(1)}, u32[]{:S(2)}, u32[]{:S(2)}) async-start(f32[128,1,128]{2,1,0:T(1,128)} %broadcast_in_dim.7), calls=%async_computation | async-start | bytes 131072 | tf_op jit(solution)/shard_map/all_to_all | solution.py:480
  13.4 0.7 compare_select_fusion
  14.1 0.8 copy.10
  15.0 0.7 reshape.57.map_ref
  15.7 2.1 %make_plan.1.plan = s32[128]{0:T(128)} custom-call(s32[1]{0:T(128)} %bitcast.tree_ref, s32[1016]{0:T(1024)} %reshape.57.map_ref), custom_call_target="tpu_custom_call" | custom-call | tf_op jit(solution)/shard_map/make_plan/pallas_call | solution.py:395
  17.8 5.2 %all-to-all-done = f32[128,1,128]{2,1,0:T(1,128)S(1)} async-done(((f32[128,1,128]{2,1,0:T(1,128)}), f32[128,1,128]{2,1,0:T(1,128)S(1)}, u32[]{:S(2)}, u32[]{:S(2)}) %all-to-all-start) | async-done | bytes 65568 | tf_op jit(solution)/shard_map/all_to_all | solution.py:480
  23.0 3.1 %gather_fusion = f32[512]{0:T(512)S(1)} fusion(f32[16384]{0:T(1024)S(1)} %bitcast.14, s32[1024]{0:T(1024)S(1)} %pad_clamp_fusion), kind=kCustom, calls=%fused_computation | custom fusion | bytes 6144 | tf_op jit(solution)/shard_map/gather | solution.py:482
  26.2 11.2 %leaf_front.1 = (f32[520,512]{1,0:T(8,128)S(1)}, f32[1312,128]{1,0:T(8,128)S(1)}) custom-call(s32[128]{0:T(128)S(1)} %copy-done.1, f32[512,512]{1,0:T(8,128)S(1)} %bitcast.12, f32[1,512]{1,0:T(1,128)S(1)} %copy-done.2, f32[1,512]{1,0:T(1,128)S(1)} %copy-done.3, f32[1,512]{1,0:T(1,128)S(1)} %bitcast.13), custom_call_target="tpu_custom_call" | custom-call | tf_op jit(solution)/shard_map/leaf_front/pallas_call | solution.py:407
  37.4 1.0 collective-permute-start
  38.5 1.7 %collective-permute-done.rest_0_ = f32[1312,128]{1,0:T(8,128)S(1)} collective-permute-done((f32[1312,128]{1,0:T(8,128)S(1)}, f32[1312,128]{1,0:T(8,128)S(1)}, u32[]{:S(2)}, u32[]{:S(2)}) %collective-permute-start) | collective-permute-done | bytes 671776 | tf_op jit(solution)/shard_map/ppermute | solution.py:468
  40.2 5.6 %merge_0.1 = (f32[128,128]{1,0:T(8,128)S(1)}, f32[128,512]{1,0:T(8,128)S(1)}, f32[8,128]{1,0:T(8,128)S(1)}, f32[520,512]{1,0:T(8,128)S(1)}, f32[656,128]{1,0:T(8,128)S(1)}) custom-call(s32[1]{0:T(128)S(6)} %and.5.core_ref, s32[128]{0:T(128)S(1)} %copy-done.1, f32[520,512]{1,0:T(8,128)S(1)} %get-tuple-element.41.own.refs_13_, ...), custom_call_target="tpu_custom_call" | custom-call | tf_op jit(solution)/shard_map/merge_0/pallas_call | solution.py:444
  45.8 1.2 collective-permute-start.1
  47.0 0.3 collective-permute-start.2
  47.3 9.0 %collective-permute-done.2.theirs = f32[128,128]{1,0:T(8,128)S(1)} collective-permute-done((f32[128,128]{1,0:T(8,128)S(1)}, f32[128,128]{1,0:T(8,128)S(1)}, u32[]{:S(2)}, u32[]{:S(2)}) %collective-permute-start.2) | collective-permute-done | bytes 65568 | tf_op jit(solution)/shard_map/ppermute | solution.py:468
  56.4 3.4 %inverse_1.1.rest_0_ = f32[128,128]{1,0:T(8,128)S(1)} custom-call(s32[128]{0:T(128)S(1)} %copy-done.1, f32[128,128]{1,0:T(8,128)S(1)} %get-tuple-element.46.own, f32[128,128]{1,0:T(8,128)S(1)} %collective-permute-done.2.theirs), custom_call_target="tpu_custom_call" | custom-call | flops 8388608 | bytes 196608 | tf_op jit(solution)/shard_map/inverse_1/pallas_call | solution.py:419
  59.8 1.3 collective-permute-start.3
  61.1 1.3 collective-permute-done.3.rest_2_
  62.4 1.8 %merge_1.1 = (f32[128,128]{1,0:T(8,128)S(1)}, f32[128,512]{1,0:T(8,128)S(1)}, f32[8,128]{1,0:T(8,128)S(1)}, f32[520,512]{1,0:T(8,128)S(1)}, f32[656,128]{1,0:T(8,128)S(1)}) custom-call(s32[1]{0:T(128)S(6)} %and.5.core_ref, s32[128]{0:T(128)S(1)} %copy-done.1, f32[520,512]{1,0:T(8,128)S(1)} %get-tuple-element.44.own, f32[128,128]{1,0:T(8,128)S(1)} %inverse_1.1.rest_0_, ...), custom_call_target="tpu_custom_call" | custom-call | tf_op jit(solution)/shard_map/merge_1/pallas_call | solution.py:444
  64.2 5.9 %collective-permute-start.4 = (f32[656,128]{1,0:T(8,128)S(1)}, f32[656,128]{1,0:T(8,128)S(1)}, u32[]{:S(2)}, u32[]{:S(2)}) collective-permute-start(f32[656,128]{1,0:T(8,128)S(1)} %get-tuple-element.51), channel_id=1, source_target_pairs={{0,64},{16,80},{32,96},{48,112},{64,0},{80,16},{96,32},{112,48},{1... | collective-permute-start | bytes 1007624 | tf_op jit(solution)/shard_map/ppermute | solution.py:468
  70.2 9.3 %collective-permute-done.5.theirs = f32[128,128]{1,0:T(8,128)S(1)} collective-permute-done((f32[128,128]{1,0:T(8,128)S(1)}, f32[128,128]{1,0:T(8,128)S(1)}, u32[]{:S(2)}, u32[]{:S(2)}) %collective-permute-start.5) | collective-permute-done | bytes 65568 | tf_op jit(solution)/shard_map/ppermute | solution.py:468
  79.5 3.4 %inverse_2.1.rest_0_ = f32[128,128]{1,0:T(8,128)S(1)} custom-call(s32[128]{0:T(128)S(1)} %copy-done.1, f32[128,128]{1,0:T(8,128)S(1)} %get-tuple-element.52.own, f32[128,128]{1,0:T(8,128)S(1)} %collective-permute-done.5.theirs), custom_call_target="tpu_custom_call" | custom-call | flops 8388608 | bytes 196608 | tf_op jit(solution)/shard_map/inverse_2/pallas_call | solution.py:419
  82.9 1.0 collective-permute-start.6
  83.9 1.3 collective-permute-done.6.rest_2_
  85.2 1.6 merge_2.1
  86.8 2.1 %collective-permute-start.7 = (f32[656,128]{1,0:T(8,128)S(1)}, f32[656,128]{1,0:T(8,128)S(1)}, u32[]{:S(2)}, u32[]{:S(2)}) collective-permute-start(f32[656,128]{1,0:T(8,128)S(1)} %get-tuple-element.57), channel_id=1, source_target_pairs={{0,1},{1,0},{2,3},{3,2},{4,5},{5,4},{6,7},{7,6},{8,9},{9,8},{10,11... | collective-permute-start | bytes 1007624 | tf_op jit(solution)/shard_map/ppermute | solution.py:468
  88.9 9.3 %collective-permute-done.8.theirs = f32[128,128]{1,0:T(8,128)S(1)} collective-permute-done((f32[128,128]{1,0:T(8,128)S(1)}, f32[128,128]{1,0:T(8,128)S(1)}, u32[]{:S(2)}, u32[]{:S(2)}) %collective-permute-start.8) | collective-permute-done | bytes 65568 | tf_op jit(solution)/shard_map/ppermute | solution.py:468
  98.2 3.4 %inverse_3.1.rest_0_ = f32[128,128]{1,0:T(8,128)S(1)} custom-call(s32[128]{0:T(128)S(1)} %copy-done.1, f32[128,128]{1,0:T(8,128)S(1)} %get-tuple-element.58.own, f32[128,128]{1,0:T(8,128)S(1)} %collective-permute-done.8.theirs), custom_call_target="tpu_custom_call" | custom-call | flops 8388608 | bytes 196608 | tf_op jit(solution)/shard_map/inverse_3/pallas_call | solution.py:419
  101.6 1.0 collective-permute-start.9
  102.6 1.3 collective-permute-done.9.rest_2_
  103.9 1.4 merge_3.1
  105.4 3.0 %collective-permute-start.11 = (f32[128,128]{1,0:T(8,128)S(1)}, f32[128,128]{1,0:T(8,128)S(1)}, u32[]{:S(2)}, u32[]{:S(2)}) collective-permute-start(f32[128,128]{1,0:T(8,128)S(1)} %get-tuple-element.64.own), channel_id=1, source_target_pairs={{0,2},{1,3},{2,0},{3,1},{4,6},{5,7},{6,4},{7,5},{8,10},{9,11},{10,... | collective-permute-start | bytes 196616 | tf_op jit(solution)/shard_map/ppermute | solution.py:468
  108.3 6.2 %collective-permute-done.11.theirs = f32[128,128]{1,0:T(8,128)S(1)} collective-permute-done((f32[128,128]{1,0:T(8,128)S(1)}, f32[128,128]{1,0:T(8,128)S(1)}, u32[]{:S(2)}, u32[]{:S(2)}) %collective-permute-start.11) | collective-permute-done | bytes 65568 | tf_op jit(solution)/shard_map/ppermute | solution.py:468
  114.5 3.4 %inverse_4.1.rest_0_ = f32[128,128]{1,0:T(8,128)S(1)} custom-call(s32[128]{0:T(128)S(1)} %copy-done.1, f32[128,128]{1,0:T(8,128)S(1)} %get-tuple-element.64.own, f32[128,128]{1,0:T(8,128)S(1)} %collective-permute-done.11.theirs), custom_call_target="tpu_custom_call" | custom-call | flops 8388608 | bytes 196608 | tf_op jit(solution)/shard_map/inverse_4/pallas_call | solution.py:419
  118.0 1.3 collective-permute-start.12
  119.3 1.1 collective-permute-done.12.rest_2_
  120.4 1.2 merge_4.1
  121.9 1.5 collective-permute-start.13
  123.3 6.2 %collective-permute-done.13.theirs = f32[128,128]{1,0:T(8,128)S(1)} collective-permute-done((f32[128,128]{1,0:T(8,128)S(1)}, f32[128,128]{1,0:T(8,128)S(1)}, u32[]{:S(2)}, u32[]{:S(2)}) %collective-permute-start.13) | collective-permute-done | bytes 65568 | tf_op jit(solution)/shard_map/ppermute | solution.py:468
  129.6 0.5 inverse_5.1.rest_0_
  130.1 0.6 merge_5.1
  130.7 3.5 %collective-permute-start.15 = (f32[136,128]{1,0:T(8,128)S(1)}, f32[136,128]{1,0:T(8,128)S(1)}, u32[]{:S(2)}, u32[]{:S(2)}) collective-permute-start(f32[136,128]{1,0:T(8,128)S(1)} %get-tuple-element.79), channel_id=1, source_target_pairs={{0,8},{1,9},{2,10},{3,11},{4,12},{5,13},{6,14},{7,15},{8,0},{9,1},... | collective-permute-start | bytes 208904 | tf_op jit(solution)/shard_map/ppermute | solution.py:468
  134.3 1.7 %collective-permute-done.15.rest_0_ = f32[136,128]{1,0:T(8,128)S(1)} collective-permute-done((f32[136,128]{1,0:T(8,128)S(1)}, f32[136,128]{1,0:T(8,128)S(1)}, u32[]{:S(2)}, u32[]{:S(2)}) %collective-permute-start.15) | collective-permute-done | bytes 69664 | tf_op jit(solution)/shard_map/ppermute | solution.py:468
  136.0 3.9 %merge_6.1.refs_12_ = f32[8,128]{1,0:T(8,128)S(1)} custom-call(s32[1]{0:T(128)S(6)} %and.5.core_ref, s32[128]{0:T(128)S(1)} %copy-done.1, f32[136,128]{1,0:T(8,128)S(1)} %get-tuple-element.78.own, f32[136,128]{1,0:T(8,128)S(1)} %collective-permute-done.15.rest_0_), custom_call_target="tpu_custom_call" | custom-call | tf_op jit(solution)/shard_map/merge_6/pallas_call | solution.py:444
  139.9 2.4 %recover.1 = f32[8,512]{1,0:T(8,128)S(1)} custom-call(s32[128]{0:T(128)S(1)} %copy-done.1, f32[128,512]{1,0:T(8,128)S(1)} %get-tuple-element.43.refs_0_, f32[128,512]{1,0:T(8,128)S(1)} %get-tuple-element.49.refs_1_, f32[128,512]{1,0:T(8,128)S(1)} %get-tuple-element.55.refs_2_, f32[128,384]{1,0:T(8,128)S(1)} %get-tuple-element.61.refs_3_, ...), custom_call_target="tpu_custom_call" | custom-call | tf_op jit(solution)/shard_map/recover/pallas_call | solution.py:456
  142.4 3.4 %scatter_custom_fusion = f32[16384]{0:T(1024)S(1)} fusion(s32[512]{0:T(512)} %bitcast.20, f32[512]{0:T(512)S(1)} %multiply_multiply_fusion, f32[]{:T(128)} %constant.19.clone.1), kind=kCustom, calls=%fused_computation.2 | custom fusion | flops 512 | bytes 66048 | tf_op jit(solution)/shard_map/scatter-add | solution.py:504
  145.8 20.0 %all_to_all.15 = f32[128,1,128]{2,1,0:T(1,128)S(1)} all-to-all(f32[128,1,128]{2,1,0:T(1,128)S(1)} %bitcast.16), channel_id=1, replica_groups=mesh['leaf'=8,'sub'=16] {'leaf','sub'}, dimensions={0} | all-to-all | bytes 131072 | tf_op jit(solution)/shard_map/all_to_all | solution.py:505
  165.8 0.5 reduce_sum.9
  (23 shorter events, 0.7 us)
Async XLA Ops:
  1.9 21.1 %all-to-all-start = ((f32[128,1,128]{2,1,0:T(1,128)}), f32[128,1,128]{2,1,0:T(1,128)S(1)}, u32[]{:S(2)}, u32[]{:S(2)}) async-start(f32[128,1,128]{2,1,0:T(1,128)} %broadcast_in_dim.7), calls=%async_computation | async-start | bytes 131072 | tf_op jit(solution)/shard_map/all_to_all | solution.py:480
  15.7 10.5 %copy-start = (f32[1,512,512]{2,1,0:T(8,128)S(1)}, f32[1,512,512]{2,1,0:T(8,128)}, u32[]{:S(2)}) copy-start(f32[1,512,512]{2,1,0:T(8,128)} %param.6) | copy-start | bytes 3145732
  15.7 10.5 %copy-start.2 = (f32[1,512]{1,0:T(1,128)S(1)}, f32[1,512]{1,0:T(1,128)}, u32[]{:S(2)}) copy-start(f32[1,512]{1,0:T(1,128)} %source.1) | copy-start | bytes 6148
  15.7 10.5 %copy-start.3 = (f32[1,512]{1,0:T(1,128)S(1)}, f32[1,512]{1,0:T(1,128)}, u32[]{:S(2)}) copy-start(f32[1,512]{1,0:T(1,128)} %observe.1) | copy-start | bytes 6148
  17.8 8.4 %copy-start.1 = (s32[128]{0:T(128)S(1)}, s32[128]{0:T(128)}, u32[]{:S(2)}) copy-start(s32[128]{0:T(128)} %make_plan.1.plan) | copy-start | bytes 1540
  37.4 2.8 %collective-permute-start = (f32[1312,128]{1,0:T(8,128)S(1)}, f32[1312,128]{1,0:T(8,128)S(1)}, u32[]{:S(2)}, u32[]{:S(2)}) collective-permute-start(f32[1312,128]{1,0:T(8,128)S(1)} %get-tuple-element.42), channel_id=1, source_target_pairs={{0,16},{16,0},{32,48},{48,32},{64,80},{80,64},{96,112},{112,96},{1... | collective-permute-start | bytes 2015240 | tf_op jit(solution)/shard_map/ppermute | solution.py:468
  45.8 14.0 %collective-permute-start.1 = (f32[656,128]{1,0:T(8,128)S(1)}, f32[656,128]{1,0:T(8,128)S(1)}, u32[]{:S(2)}, u32[]{:S(2)}) collective-permute-start(f32[656,128]{1,0:T(8,128)S(1)} %get-tuple-element.45), channel_id=1, source_target_pairs={{0,32},{16,48},{32,0},{48,16},{64,96},{80,112},{96,64},{112,80},{1... | collective-permute-start | bytes 1007624 | tf_op jit(solution)/shard_map/ppermute | solution.py:468
  47.0 9.4 %collective-permute-start.2 = (f32[128,128]{1,0:T(8,128)S(1)}, f32[128,128]{1,0:T(8,128)S(1)}, u32[]{:S(2)}, u32[]{:S(2)}) collective-permute-start(f32[128,128]{1,0:T(8,128)S(1)} %get-tuple-element.46.own), channel_id=1, source_target_pairs={{0,32},{16,48},{32,0},{48,16},{64,96},{80,112},{96,64},{112,80},{1... | collective-permute-start | bytes 196616 | tf_op jit(solution)/shard_map/ppermute | solution.py:468
  59.8 2.6 %collective-permute-start.3 = (f32[656,128]{1,0:T(8,128)S(1)}, f32[656,128]{1,0:T(8,128)S(1)}, u32[]{:S(2)}, u32[]{:S(2)}) collective-permute-start(f32[656,128]{1,0:T(8,128)S(1)} %collective-permute-done.1.rest_1_), channel_id=1, source_target_pairs={{0,16},{16,0},{32,48},{48,32},{64,80},{80,64},{96,112},{112,96},{1... | collective-permute-start | bytes 1007624 | tf_op jit(solution)/shard_map/ppermute | solution.py:468
  64.2 18.7 %collective-permute-start.4 = (f32[656,128]{1,0:T(8,128)S(1)}, f32[656,128]{1,0:T(8,128)S(1)}, u32[]{:S(2)}, u32[]{:S(2)}) collective-permute-start(f32[656,128]{1,0:T(8,128)S(1)} %get-tuple-element.51), channel_id=1, source_target_pairs={{0,64},{16,80},{32,96},{48,112},{64,0},{80,16},{96,32},{112,48},{1... | collective-permute-start | bytes 1007624 | tf_op jit(solution)/shard_map/ppermute | solution.py:468
  70.1 9.4 %collective-permute-start.5 = (f32[128,128]{1,0:T(8,128)S(1)}, f32[128,128]{1,0:T(8,128)S(1)}, u32[]{:S(2)}, u32[]{:S(2)}) collective-permute-start(f32[128,128]{1,0:T(8,128)S(1)} %get-tuple-element.52.own), channel_id=1, source_target_pairs={{0,64},{16,80},{32,96},{48,112},{64,0},{80,16},{96,32},{112,48},{1... | collective-permute-start | bytes 196616 | tf_op jit(solution)/shard_map/ppermute | solution.py:468
  82.9 2.2 %collective-permute-start.6 = (f32[656,128]{1,0:T(8,128)S(1)}, f32[656,128]{1,0:T(8,128)S(1)}, u32[]{:S(2)}, u32[]{:S(2)}) collective-permute-start(f32[656,128]{1,0:T(8,128)S(1)} %collective-permute-done.4.rest_1_), channel_id=1, source_target_pairs={{0,16},{16,0},{32,48},{48,32},{64,80},{80,64},{96,112},{112,96},{1... | collective-permute-start | bytes 1007624 | tf_op jit(solution)/shard_map/ppermute | solution.py:468
  86.8 14.9 %collective-permute-start.7 = (f32[656,128]{1,0:T(8,128)S(1)}, f32[656,128]{1,0:T(8,128)S(1)}, u32[]{:S(2)}, u32[]{:S(2)}) collective-permute-start(f32[656,128]{1,0:T(8,128)S(1)} %get-tuple-element.57), channel_id=1, source_target_pairs={{0,1},{1,0},{2,3},{3,2},{4,5},{5,4},{6,7},{7,6},{8,9},{9,8},{10,11... | collective-permute-start | bytes 1007624 | tf_op jit(solution)/shard_map/ppermute | solution.py:468
  88.8 9.4 %collective-permute-start.8 = (f32[128,128]{1,0:T(8,128)S(1)}, f32[128,128]{1,0:T(8,128)S(1)}, u32[]{:S(2)}, u32[]{:S(2)}) collective-permute-start(f32[128,128]{1,0:T(8,128)S(1)} %get-tuple-element.58.own), channel_id=1, source_target_pairs={{0,1},{1,0},{2,3},{3,2},{4,5},{5,4},{6,7},{7,6},{8,9},{9,8},{10,11... | collective-permute-start | bytes 196616 | tf_op jit(solution)/shard_map/ppermute | solution.py:468
  101.6 2.2 %collective-permute-start.9 = (f32[656,128]{1,0:T(8,128)S(1)}, f32[656,128]{1,0:T(8,128)S(1)}, u32[]{:S(2)}, u32[]{:S(2)}) collective-permute-start(f32[656,128]{1,0:T(8,128)S(1)} %collective-permute-done.7.rest_1_), channel_id=1, source_target_pairs={{0,16},{16,0},{32,48},{48,32},{64,80},{80,64},{96,112},{112,96},{1... | collective-permute-start | bytes 1007624 | tf_op jit(solution)/shard_map/ppermute | solution.py:468
  105.3 12.7 %collective-permute-start.10 = (f32[400,128]{1,0:T(8,128)S(1)}, f32[400,128]{1,0:T(8,128)S(1)}, u32[]{:S(2)}, u32[]{:S(2)}) collective-permute-start(f32[400,128]{1,0:T(8,128)S(1)} %get-tuple-element.63), channel_id=1, source_target_pairs={{0,2},{1,3},{2,0},{3,1},{4,6},{5,7},{6,4},{7,5},{8,10},{9,11},{10,... | collective-permute-start | bytes 614408 | tf_op jit(solution)/shard_map/ppermute | solution.py:468
  105.4 9.2 %collective-permute-start.11 = (f32[128,128]{1,0:T(8,128)S(1)}, f32[128,128]{1,0:T(8,128)S(1)}, u32[]{:S(2)}, u32[]{:S(2)}) collective-permute-start(f32[128,128]{1,0:T(8,128)S(1)} %get-tuple-element.64.own), channel_id=1, source_target_pairs={{0,2},{1,3},{2,0},{3,1},{4,6},{5,7},{6,4},{7,5},{8,10},{9,11},{10,... | collective-permute-start | bytes 196616 | tf_op jit(solution)/shard_map/ppermute | solution.py:468
  118.0 2.4 %collective-permute-start.12 = (f32[400,128]{1,0:T(8,128)S(1)}, f32[400,128]{1,0:T(8,128)S(1)}, u32[]{:S(2)}, u32[]{:S(2)}) collective-permute-start(f32[400,128]{1,0:T(8,128)S(1)} %collective-permute-done.10.rest_1_), channel_id=1, source_target_pairs={{0,16},{16,0},{32,48},{48,32},{64,80},{80,64},{96,112},{112,96},{1... | collective-permute-start | bytes 614408 | tf_op jit(solution)/shard_map/ppermute | solution.py:468
  121.6 8.6 %collective-permute-start.14 = (f32[400,128]{1,0:T(8,128)S(1)}, f32[400,128]{1,0:T(8,128)S(1)}, u32[]{:S(2)}, u32[]{:S(2)}) collective-permute-start(f32[400,128]{1,0:T(8,128)S(1)} %get-tuple-element.70), channel_id=1, source_target_pairs={{0,4},{1,5},{2,6},{3,7},{4,0},{5,1},{6,2},{7,3},{8,12},{9,13},{10,... | collective-permute-start | bytes 614408 | tf_op jit(solution)/shard_map/ppermute | solution.py:468
  121.9 7.7 %collective-permute-start.13 = (f32[128,128]{1,0:T(8,128)S(1)}, f32[128,128]{1,0:T(8,128)S(1)}, u32[]{:S(2)}, u32[]{:S(2)}) collective-permute-start(f32[128,128]{1,0:T(8,128)S(1)} %get-tuple-element.69.own), channel_id=1, source_target_pairs={{0,4},{1,5},{2,6},{3,7},{4,0},{5,1},{6,2},{7,3},{8,12},{9,13},{10,... | collective-permute-start | bytes 196616 | tf_op jit(solution)/shard_map/ppermute | solution.py:468
  130.7 5.2 %collective-permute-start.15 = (f32[136,128]{1,0:T(8,128)S(1)}, f32[136,128]{1,0:T(8,128)S(1)}, u32[]{:S(2)}, u32[]{:S(2)}) collective-permute-start(f32[136,128]{1,0:T(8,128)S(1)} %get-tuple-element.79), channel_id=1, source_target_pairs={{0,8},{1,9},{2,10},{3,11},{4,12},{5,13},{6,14},{7,15},{8,0},{9,1},... | collective-permute-start | bytes 208904 | tf_op jit(solution)/shard_map/ppermute | solution.py:468
  142.3 24.0 %copy-start.4 = (f32[1,512]{1,0:T(1,128)}, f32[1,512]{1,0:T(1,128)S(1)}, u32[]{:S(2)}) copy-start(f32[1,512]{1,0:T(1,128)S(1)} %get-tuple-element.81) | copy-start | bytes 6148

commit v2 on v1

--- a/solution.py
+++ b/solution.py
@@ -8,6 +8,7 @@
 from jax.sharding import PartitionSpec as P
 
 BW = 128
+BW_BITS = 7
 NB = 4
 KEEP = NB - 1
 FW = NB * BW
@@ -20,6 +21,17 @@
 def split(x):
     high = x.astype(jnp.bfloat16)
     return high, (x - high.astype(jnp.float32)).astype(jnp.bfloat16)
+
+
+def split_exact(x):
+    high, low = split(x)
+    rest = x - high.astype(jnp.float32)
+    return high, low, (rest - low.astype(jnp.float32)).astype(jnp.bfloat16)
+
+
+def one_hot(cells, width):
+    row = lax.broadcasted_iota(jnp.int32, (width, cells.shape[1]), 0)
+    return row == jnp.broadcast_to(cells, row.shape)
 
 
 def dot_split(a, b):
@@ -216,7 +228,14 @@
         plan[level * STRIDE + 8] = jnp.where(plan[level * STRIDE] == dropped, 1, 0)
 
 
-def leaf_kernel(levels, plan, leaf, source, observe, perm, front, pack, inverse, wide, buffer):
+def leaf_kernel(levels, plan, leaf, source, observe, zones, cells, front, pack, perm, inverse, wide, buffer):
+    owner = one_hot(cells[...] >> BW_BITS, zones.shape[0]).astype(jnp.float32).astype(jnp.bfloat16)
+    held = sum(
+        lax.dot_general(part, owner, (((0,), (0,)), ((), ())), preferred_element_type=jnp.float32)
+        for part in split_exact(zones[...])
+    )
+    within = one_hot(cells[...] & (BW - 1), BW)
+    perm[...] = jnp.exp(jnp.sum(jnp.where(within, held, 0.0), axis=0, keepdims=True))
     front[0:FW, :] = leaf[...]
     eye = lax.broadcasted_iota(jnp.int32, (BW, BW), 0) == lax.broadcasted_iota(jnp.int32, (BW, BW), 1)
     for i in range(NB):
@@ -252,7 +271,7 @@
 
 
 def early(levels, level):
-    return 0 < level < levels - 1
+    return False
 
 
 def merge_kernel(levels, level, core_ref, plan, own, *rest):
@@ -364,7 +383,7 @@
 
 def recover_kernel(levels, plan, *refs):
     couplings, reduced = refs[: levels - 1], refs[levels - 1 : 2 * levels - 1]
-    leaf, out = refs[2 * levels - 1 :]
+    leaf, perm, cells, out, partial = refs[2 * levels - 1 :]
     solved = [reduced[levels - 1][...]]
     for level in reversed(range(1, levels)):
         kept = [pick(solved, plan[level * STRIDE + a]) for a in range(active(levels, level))]
@@ -373,9 +392,18 @@
     spots = [plan[levels * STRIDE + 4 + i] for i in range(NB)]
     kept = [pick(solved, jnp.where(spot >= 0, plan[jnp.maximum(spot, 0)], -1)) for spot in spots]
     new = dot_split(split(jnp.concatenate(kept, 1)), split(leaf[0:FW, :])) - leaf[FW : FW + 8, :]
-    for i in range(NB):
-        at = slice(i * BW, i * BW + BW)
-        out[:, at] = jnp.where(spots[i] >= 0, kept[i], new[:, at])
+    both = jnp.concatenate(
+        [jnp.where(spots[i] >= 0, kept[i], new[:, i * BW : i * BW + BW]) for i in range(NB)], 1
+    )
+    out[...] = both[0:1]
+    terms = -perm[...] * both[0:1] * both[1:2]
+    owner = one_hot(cells[...] >> BW_BITS, partial.shape[0]).astype(jnp.float32).astype(jnp.bfloat16)
+    within = one_hot(cells[...] & (BW - 1), BW)
+    spread = jnp.where(within, jnp.broadcast_to(terms, within.shape), 0.0)
+    partial[...] = sum(
+        lax.dot_general(owner, part, (((1,), (1,)), ((), ())), preferred_element_type=jnp.float32)
+        for part in split_exact(spread)
+    )
 
 
 SCALARS = pl.BlockSpec(memory_space=pltpu.SMEM)
@@ -402,17 +430,17 @@
     )(tree, maps)
 
 
-def leaf_front(levels, plan, leaf, source, observe, perm):
+def leaf_front(levels, plan, leaf, source, observe, zones, cells):
     count = active(levels, 0)
     return pl.pallas_call(
         functools.partial(leaf_kernel, levels),
-        out_shape=(f32(FW + 8, FW), f32(parts(count) * part_rows(count), BW)),
-        in_specs=[SCALARS] + [WHOLE] * 4,
-        out_specs=(WHOLE, WHOLE),
+        out_shape=(f32(FW + 8, FW), f32(parts(count) * part_rows(count), BW), f32(1, FW)),
+        in_specs=[SCALARS] + [WHOLE] * 5,
+        out_specs=(WHOLE,) * 3,
         scratch_shapes=[vmem(BW, BW), vmem(BW, FW), vmem(8 * SLOTS, BW)],
         compiler_params=PARAMS,
         name="leaf_front",
-    )(plan, leaf, source, observe, perm)
+    )(plan, leaf, source, observe, zones, cells)
 
 
 def shared_inverse(level, plan, own, theirs):
@@ -452,15 +480,15 @@
     )(core, plan, own, *ahead, *theirs)
 
 
-def recover(levels, plan, couplings, reduced, leaf):
+def recover(levels, plan, couplings, reduced, leaf, perm, cells):
     return pl.pallas_call(
         functools.partial(recover_kernel, levels),
-        out_shape=f32(8, FW),
-        in_specs=[SCALARS] + [WHOLE] * (2 * levels),
-        out_specs=WHOLE,
+        out_shape=(f32(1, FW), f32(1 << levels, BW)),
+        in_specs=[SCALARS] + [WHOLE] * (2 * levels + 2),
+        out_specs=(WHOLE, WHOLE),
         compiler_params=PARAMS,
         name="recover",
-    )(plan, *couplings, *reduced, leaf)
+    )(plan, *couplings, *reduced, leaf, perm, cells)
 
 
 def partner(block, axis, bit):
@@ -477,10 +505,8 @@
     core = tree & 1
     plan = make_plan(levels, tree, block_map.reshape(-1))
     zones = jnp.broadcast_to(log_perm[None], (devices, log_perm.shape[0]))
-    all_zones = lax.all_to_all(zones, ("leaf", "sub"), 0, 0, tiled=True).reshape(-1)
-    cells = zone_ids[0]
-    perm = jnp.exp(all_zones[cells])
-    leaf, pack = leaf_front(levels, plan, leaf_matrix[0], leaf_source, observe, perm[None])
+    all_zones = lax.all_to_all(zones, ("leaf", "sub"), 0, 0, tiled=True)
+    leaf, pack, perm = leaf_front(levels, plan, leaf_matrix[0], leaf_source, observe, all_zones, zone_ids)
     front, couplings, reduced = leaf, [], []
     for level in range(levels):
         axis, bit = ("leaf", level) if level < leaf_bits else ("sub", level - leaf_bits)
@@ -499,11 +525,9 @@
             *more, front, pack = more
         couplings += more[:-1]
         reduced += more[-1:]
-    solution = recover(levels, plan, couplings, reduced, leaf)
-    terms = -perm * solution[0] * solution[1]
-    partial = jax.ops.segment_sum(terms, cells, num_segments=all_zones.shape[0])
-    shares = lax.all_to_all(partial.reshape(devices, -1), ("leaf", "sub"), 0, 0, tiled=True)
-    return solution[0][None, :], shares.sum(0)
+    solution, partial = recover(levels, plan, couplings, reduced, leaf, perm, zone_ids)
+    shares = lax.all_to_all(partial, ("leaf", "sub"), 0, 0, tiled=True)
+    return solution, shares.sum(0)
 
 
 def solution(mesh):

time: 166 us -> 159 us (0.958)
  starting transfers between devices: 35.1 us -> 21.6 us
  Pallas kernels: 46.1 us -> 53.7 us
  waiting for transfers between devices: 53.6 us -> 59.5 us
  blocking collectives: 20 us -> 14.8 us
  other arithmetic: 4.66 us -> 0.66 us
    pallas_call x7, Pallas kernels: 16.1 us -> 32 us  [merge(): pl.pallas_call(functools.partial(merge_kernel, levels, level), out_shape=...]
    pallas_call x6 -> x1, Pallas kernels: 16.7 us -> 3.1 us  [recover(): pl.pallas_call(functools.partial(recover_kernel, levels), out_shape=(f32(...]
    ppermute x16 -> x11, starting transfers between devices: 23.6 us -> 10.1 us  [partner(): return lax.ppermute(block, axis, [(k, k ^ 1 << bit) for k in range(count)])]
    pallas_call x1, Pallas kernels: 11.2 us -> 16.7 us  [leaf_front(): pl.pallas_call(functools.partial(leaf_kernel, levels), out_shape=(f32(FW...]
    all_to_all x1, blocking collectives: 20 us -> 14.8 us  [shards(): shares = lax.all_to_all(partial, ('leaf', 'sub'), 0, 0, tiled=True)]
    ppermute x16 -> x11, waiting for transfers between devices: 48.4 us -> 53.5 us  [partner(): return lax.ppermute(block, axis, [(k, k ^ 1 << bit) for k in range(count)])]
    unnamed x11 -> x13, local copies, waits for them, and re-layouts: 0.84 us -> 4.74 us
    scatter-add x1 -> x0, other arithmetic: 3.42 us -> none  [shards(): partial = jax.ops.segment_sum(terms, cells, num_segments=all_zones.shape[0])]
  transfers between devices with their start and end apart: 17 -> 12, of which waited for: 12 -> 12; matrix products, arithmetic and copies ran while one was open for 1% -> 1% of each run, Pallas kernels for 10% -> 1%
where the time goes in v2:
time: 159 us; the launch traced here: 158 us
  waiting for transfers between devices  59.5 us (37%)
  Pallas kernels  53.7 us (34%)
  starting transfers between devices  21.6 us (14%)
  blocking collectives  14.8 us (9%)
  local copies, waits for them, and re-layouts  6.77 us (4%)
    ppermute x11, waiting for transfers between devices, partner(): return lax.ppermute(block, axis, [(k, k ^ 1 << bit) for k in range(count)])  53.5 us
    pallas_call x7, Pallas kernels, merge(): pl.pallas_call(functools.partial(merge_kernel, levels, level), out_shape=...  32 us
    pallas_call x1, Pallas kernels, leaf_front(): pl.pallas_call(functools.partial(leaf_kernel, levels), out_shape=(f32(FW...  16.7 us
    all_to_all x1, blocking collectives, shards(): shares = lax.all_to_all(partial, ('leaf', 'sub'), 0, 0, tiled=True)  14.8 us
    all_to_all x1, starting transfers between devices, shards(): all_zones = lax.all_to_all(zones, ('leaf', 'sub'), 0, 0, tiled=True)  11.5 us
    ppermute x11, starting transfers between devices, partner(): return lax.ppermute(block, axis, [(k, k ^ 1 << bit) for k in range(count)])  10.1 us
    all_to_all x1, waiting for transfers between devices, shards(): all_zones = lax.all_to_all(zones, ('leaf', 'sub'), 0, 0, tiled=True)  6.03 us
    unnamed x13, local copies, waits for them, and re-layouts  4.74 us
  transfers between devices with their start and end apart: 12, of which 12 were waited for; matrix products, arithmetic and copies ran while one was open for 1% of the time, Pallas kernels for 1%

profile of v2, /device:TPU:1, one launch (start us, length us, event | category | flops | bytes accessed | tf_op | source)
XLA Modules:
  0.0 157.8 jit_solution(9582835475855880423)
XLA Ops:
  0.6 1.3 broadcast_in_dim.10
  1.9 11.5 %all-to-all-start = ((f32[128,1,128]{2,1,0:T(1,128)}), f32[128,1,128]{2,1,0:T(1,128)S(1)}, u32[]{:S(2)}, u32[]{:S(2)}) async-start(f32[128,1,128]{2,1,0:T(1,128)} %broadcast_in_dim.10), calls=%async_computation | async-start | bytes 131072 | tf_op jit(solution)/shard_map/all_to_all | solution.py:508
  13.5 0.8 copy.9
  14.3 0.7 reshape.15.map_ref
  15.0 2.0 %make_plan.1.plan = s32[128]{0:T(128)} custom-call(s32[1]{0:T(128)} %bitcast.tree_ref, s32[1016]{0:T(1024)} %reshape.15.map_ref), custom_call_target="tpu_custom_call" | custom-call | tf_op jit(solution)/shard_map/make_plan/pallas_call | solution.py:423
  17.0 6.0 %all-to-all-done = f32[128,1,128]{2,1,0:T(1,128)S(1)} async-done(((f32[128,1,128]{2,1,0:T(1,128)}), f32[128,1,128]{2,1,0:T(1,128)S(1)}, u32[]{:S(2)}, u32[]{:S(2)}) %all-to-all-start) | async-done | bytes 65568 | tf_op jit(solution)/shard_map/all_to_all | solution.py:508
  23.0 0.0 copy-start
  23.0 1.2 copy-done
  24.2 0.0 copy-start.1
  24.2 0.7 copy-done.1
  24.9 0.7 copy-done.2
  25.6 0.7 copy-done.4
  26.3 0.7 copy-done.5
  26.9 16.7 %leaf_front.1 = (f32[520,512]{1,0:T(8,128)S(1)}, f32[1312,128]{1,0:T(8,128)S(1)}, f32[1,512]{1,0:T(1,128)S(1)}) custom-call(s32[128]{0:T(128)S(1)} %copy-done.1, f32[512,512]{1,0:T(8,128)S(1)} %bitcast.6, f32[1,512]{1,0:T(1,128)S(1)} %copy-done.4, f32[1,512]{1,0:T(1,128)S(1)} %copy-done.5, f32[128,128]{1,0:T(8,128)S(1)} %bitcast.7, s32[1,512]{1,0:T(1,128)S(1)} %copy-done.2), custom_call_target="tpu_custom_call" | custom-call | tf_op jit(solution)/shard_map/leaf_front/pallas_call | solution.py:435
  43.6 0.1 collective-permute-start
  43.7 2.1 %collective-permute-done.rest_0_ = f32[1312,128]{1,0:T(8,128)S(1)} collective-permute-done((f32[1312,128]{1,0:T(8,128)S(1)}, f32[1312,128]{1,0:T(8,128)S(1)}, u32[]{:S(2)}, u32[]{:S(2)}) %collective-permute-start) | collective-permute-done | bytes 671776 | tf_op jit(solution)/shard_map/ppermute | solution.py:496
  45.8 1.0 merge_0.1
  46.8 5.2 %collective-permute-start.1 = (f32[656,128]{1,0:T(8,128)S(1)}, f32[656,128]{1,0:T(8,128)S(1)}, u32[]{:S(2)}, u32[]{:S(2)}) collective-permute-start(f32[656,128]{1,0:T(8,128)S(1)} %get-tuple-element.35), channel_id=1, source_target_pairs={{0,32},{16,48},{32,0},{48,16},{64,96},{80,112},{96,64},{112,80},{1... | collective-permute-start | bytes 1007624 | tf_op jit(solution)/shard_map/ppermute | solution.py:496
  52.0 8.1 %collective-permute-done.1.rest_0_ = f32[656,128]{1,0:T(8,128)S(1)} collective-permute-done((f32[656,128]{1,0:T(8,128)S(1)}, f32[656,128]{1,0:T(8,128)S(1)}, u32[]{:S(2)}, u32[]{:S(2)}) %collective-permute-start.1) | collective-permute-done | bytes 335904 | tf_op jit(solution)/shard_map/ppermute | solution.py:496
  60.1 0.7 collective-permute-start.2
  60.8 1.3 collective-permute-done.2.rest_1_
  62.1 5.7 %merge_1.1 = (f32[128,512]{1,0:T(8,128)S(1)}, f32[8,128]{1,0:T(8,128)S(1)}, f32[520,512]{1,0:T(8,128)S(1)}, f32[656,128]{1,0:T(8,128)S(1)}) custom-call(s32[1]{0:T(128)S(6)} %and.5.core_ref, s32[128]{0:T(128)S(1)} %copy-done.1, f32[520,512]{1,0:T(8,128)S(1)} %get-tuple-element.34.own, f32[656,128]{1,0:T(8,128)S(1)} %collective-permute-done.1.rest_0_, ...), custom_call_target="tpu_custom_call" | custom-call | tf_op jit(solution)/shard_map/merge_1/pallas_call | solution.py:472
  67.8 0.1 collective-permute-start.3
  67.9 10.6 %collective-permute-done.3.rest_0_ = f32[656,128]{1,0:T(8,128)S(1)} collective-permute-done((f32[656,128]{1,0:T(8,128)S(1)}, f32[656,128]{1,0:T(8,128)S(1)}, u32[]{:S(2)}, u32[]{:S(2)}) %collective-permute-start.3) | collective-permute-done | bytes 335904 | tf_op jit(solution)/shard_map/ppermute | solution.py:496
  78.5 1.2 collective-permute-start.4
  79.7 1.3 collective-permute-done.4.rest_1_
  81.0 5.6 %merge_2.1 = (f32[128,512]{1,0:T(8,128)S(1)}, f32[8,128]{1,0:T(8,128)S(1)}, f32[520,512]{1,0:T(8,128)S(1)}, f32[656,128]{1,0:T(8,128)S(1)}) custom-call(s32[1]{0:T(128)S(6)} %and.5.core_ref, s32[128]{0:T(128)S(1)} %copy-done.1, f32[520,512]{1,0:T(8,128)S(1)} %get-tuple-element.37.own, f32[656,128]{1,0:T(8,128)S(1)} %collective-permute-done.3.rest_0_, ...), custom_call_target="tpu_custom_call" | custom-call | tf_op jit(solution)/shard_map/merge_2/pallas_call | solution.py:472
  86.7 0.1 collective-permute-start.5
  86.7 9.1 %collective-permute-done.5.rest_0_ = f32[656,128]{1,0:T(8,128)S(1)} collective-permute-done((f32[656,128]{1,0:T(8,128)S(1)}, f32[656,128]{1,0:T(8,128)S(1)}, u32[]{:S(2)}, u32[]{:S(2)}) %collective-permute-start.5) | collective-permute-done | bytes 335904 | tf_op jit(solution)/shard_map/ppermute | solution.py:496
  95.8 1.2 collective-permute-start.6
  97.0 1.3 collective-permute-done.6.rest_1_
  98.3 5.4 %merge_3.1 = (f32[128,384]{1,0:T(8,128)S(1)}, f32[8,128]{1,0:T(8,128)S(1)}, f32[392,384]{1,0:T(8,128)S(1)}, f32[400,128]{1,0:T(8,128)S(1)}) custom-call(s32[1]{0:T(128)S(6)} %and.5.core_ref, s32[128]{0:T(128)S(1)} %copy-done.1, f32[520,512]{1,0:T(8,128)S(1)} %get-tuple-element.40.own, f32[656,128]{1,0:T(8,128)S(1)} %collective-permute-done.5.rest_0_, ...), custom_call_target="tpu_custom_call" | custom-call | tf_op jit(solution)/shard_map/merge_3/pallas_call | solution.py:472
  103.7 0.0 copy-start.3
  103.7 0.1 collective-permute-start.7
  103.8 7.8 %collective-permute-done.7.rest_0_ = f32[400,128]{1,0:T(8,128)S(1)} collective-permute-done((f32[400,128]{1,0:T(8,128)S(1)}, f32[400,128]{1,0:T(8,128)S(1)}, u32[]{:S(2)}, u32[]{:S(2)}) %collective-permute-start.7) | collective-permute-done | bytes 204832 | tf_op jit(solution)/shard_map/ppermute | solution.py:496
  111.6 1.2 collective-permute-start.8
  112.8 1.1 collective-permute-done.8.rest_1_
  113.9 5.4 %merge_4.1 = (f32[128,256]{1,0:T(8,128)S(1)}, f32[8,128]{1,0:T(8,128)S(1)}, f32[264,256]{1,0:T(8,128)S(1)}, f32[400,128]{1,0:T(8,128)S(1)}) custom-call(s32[1]{0:T(128)S(6)} %and.5.core_ref, s32[128]{0:T(128)S(1)} %copy-done.1, f32[392,384]{1,0:T(8,128)S(1)} %get-tuple-element.43.own, f32[400,128]{1,0:T(8,128)S(1)} %collective-permute-done.7.rest_0_, ...), custom_call_target="tpu_custom_call" | custom-call | tf_op jit(solution)/shard_map/merge_4/pallas_call | solution.py:472
  119.3 0.1 collective-permute-start.9
  119.4 6.3 %collective-permute-done.9.rest_0_ = f32[400,128]{1,0:T(8,128)S(1)} collective-permute-done((f32[400,128]{1,0:T(8,128)S(1)}, f32[400,128]{1,0:T(8,128)S(1)}, u32[]{:S(2)}, u32[]{:S(2)}) %collective-permute-start.9) | collective-permute-done | bytes 204832 | tf_op jit(solution)/shard_map/ppermute | solution.py:496
  125.6 4.9 %merge_5.1 = (f32[128,128]{1,0:T(8,128)S(1)}, f32[8,128]{1,0:T(8,128)S(1)}, f32[136,128]{1,0:T(8,128)S(1)}, f32[136,128]{1,0:T(8,128)S(1)}) custom-call(s32[1]{0:T(128)S(6)} %and.5.core_ref, s32[128]{0:T(128)S(1)} %copy-done.1, f32[264,256]{1,0:T(8,128)S(1)} %get-tuple-element.46.own, f32[400,128]{1,0:T(8,128)S(1)} %collective-permute-done.9.rest_0_), custom_call_target="tpu_custom_call" | custom-call | tf_op jit(solution)/shard_map/merge_5/pallas_call | solution.py:472
  130.6 0.1 collective-permute-start.10
  130.7 4.7 %collective-permute-done.10.rest_0_ = f32[136,128]{1,0:T(8,128)S(1)} collective-permute-done((f32[136,128]{1,0:T(8,128)S(1)}, f32[136,128]{1,0:T(8,128)S(1)}, u32[]{:S(2)}, u32[]{:S(2)}) %collective-permute-start.10) | collective-permute-done | bytes 69664 | tf_op jit(solution)/shard_map/ppermute | solution.py:496
  135.3 3.9 %merge_6.1.refs_12_ = f32[8,128]{1,0:T(8,128)S(1)} custom-call(s32[1]{0:T(128)S(6)} %and.5.core_ref, s32[128]{0:T(128)S(1)} %copy-done.1, f32[136,128]{1,0:T(8,128)S(1)} %get-tuple-element.55.own, f32[136,128]{1,0:T(8,128)S(1)} %collective-permute-done.10.rest_0_), custom_call_target="tpu_custom_call" | custom-call | tf_op jit(solution)/shard_map/merge_6/pallas_call | solution.py:472
  139.2 0.0 copy-done.3
  139.2 3.1 %recover.1 = (f32[1,512]{1,0:T(1,128)}, f32[128,128]{1,0:T(8,128)S(1)}) custom-call(s32[128]{0:T(128)S(1)} %copy-done.1, f32[128,512]{1,0:T(8,128)S(1)} %get-tuple-element.33.refs_0_, f32[128,512]{1,0:T(8,128)S(1)} %get-tuple-element.36.refs_1_, f32[128,512]{1,0:T(8,128)S(1)} %get-tuple-element.39.refs_2_, f32[128,384]{1,0:T(8,128)S(1)} %get-tuple-element.42.refs_3_, ...), custom_call_target="tpu_custom_call" | custom-call | tf_op jit(solution)/shard_map/recover/pallas_call | solution.py:484
  142.3 14.8 %all_to_all.17 = f32[128,1,128]{2,1,0:T(1,128)S(1)} all-to-all(f32[128,1,128]{2,1,0:T(1,128)S(1)} %bitcast.8), channel_id=1, replica_groups=mesh['leaf'=8,'sub'=16] {'leaf','sub'}, dimensions={0} | all-to-all | bytes 131072 | tf_op jit(solution)/shard_map/all_to_all | solution.py:529
  157.1 0.7 reduce_sum.9
  (3 shorter events, 0.0 us)
Async XLA Ops:
  1.9 21.1 %all-to-all-start = ((f32[128,1,128]{2,1,0:T(1,128)}), f32[128,1,128]{2,1,0:T(1,128)S(1)}, u32[]{:S(2)}, u32[]{:S(2)}) async-start(f32[128,1,128]{2,1,0:T(1,128)} %broadcast_in_dim.10), calls=%async_computation | async-start | bytes 131072 | tf_op jit(solution)/shard_map/all_to_all | solution.py:508
  23.0 1.2 copy-start
  24.2 0.7 copy-start.1
  24.9 0.7 copy-start.2
  25.6 0.7 copy-start.4
  26.3 0.7 copy-start.5
  43.6 2.2 %collective-permute-start = (f32[1312,128]{1,0:T(8,128)S(1)}, f32[1312,128]{1,0:T(8,128)S(1)}, u32[]{:S(2)}, u32[]{:S(2)}) collective-permute-start(f32[1312,128]{1,0:T(8,128)S(1)} %get-tuple-element.32), channel_id=1, source_target_pairs={{0,16},{16,0},{32,48},{48,32},{64,80},{80,64},{96,112},{112,96},{1... | collective-permute-start | bytes 2015240 | tf_op jit(solution)/shard_map/ppermute | solution.py:496
  46.8 13.3 %collective-permute-start.1 = (f32[656,128]{1,0:T(8,128)S(1)}, f32[656,128]{1,0:T(8,128)S(1)}, u32[]{:S(2)}, u32[]{:S(2)}) collective-permute-start(f32[656,128]{1,0:T(8,128)S(1)} %get-tuple-element.35), channel_id=1, source_target_pairs={{0,32},{16,48},{32,0},{48,16},{64,96},{80,112},{96,64},{112,80},{1... | collective-permute-start | bytes 1007624 | tf_op jit(solution)/shard_map/ppermute | solution.py:496
  60.1 2.0 %collective-permute-start.2 = (f32[656,128]{1,0:T(8,128)S(1)}, f32[656,128]{1,0:T(8,128)S(1)}, u32[]{:S(2)}, u32[]{:S(2)}) collective-permute-start(f32[656,128]{1,0:T(8,128)S(1)} %collective-permute-done.1.rest_0_), channel_id=1, source_target_pairs={{0,16},{16,0},{32,48},{48,32},{64,80},{80,64},{96,112},{112,96},{1... | collective-permute-start | bytes 1007624 | tf_op jit(solution)/shard_map/ppermute | solution.py:496
  67.8 10.7 %collective-permute-start.3 = (f32[656,128]{1,0:T(8,128)S(1)}, f32[656,128]{1,0:T(8,128)S(1)}, u32[]{:S(2)}, u32[]{:S(2)}) collective-permute-start(f32[656,128]{1,0:T(8,128)S(1)} %get-tuple-element.38), channel_id=1, source_target_pairs={{0,64},{16,80},{32,96},{48,112},{64,0},{80,16},{96,32},{112,48},{1... | collective-permute-start | bytes 1007624 | tf_op jit(solution)/shard_map/ppermute | solution.py:496
  78.5 2.5 %collective-permute-start.4 = (f32[656,128]{1,0:T(8,128)S(1)}, f32[656,128]{1,0:T(8,128)S(1)}, u32[]{:S(2)}, u32[]{:S(2)}) collective-permute-start(f32[656,128]{1,0:T(8,128)S(1)} %collective-permute-done.3.rest_0_), channel_id=1, source_target_pairs={{0,16},{16,0},{32,48},{48,32},{64,80},{80,64},{96,112},{112,96},{1... | collective-permute-start | bytes 1007624 | tf_op jit(solution)/shard_map/ppermute | solution.py:496
  86.7 9.2 %collective-permute-start.5 = (f32[656,128]{1,0:T(8,128)S(1)}, f32[656,128]{1,0:T(8,128)S(1)}, u32[]{:S(2)}, u32[]{:S(2)}) collective-permute-start(f32[656,128]{1,0:T(8,128)S(1)} %get-tuple-element.41), channel_id=1, source_target_pairs={{0,1},{1,0},{2,3},{3,2},{4,5},{5,4},{6,7},{7,6},{8,9},{9,8},{10,11... | collective-permute-start | bytes 1007624 | tf_op jit(solution)/shard_map/ppermute | solution.py:496
  95.8 2.5 %collective-permute-start.6 = (f32[656,128]{1,0:T(8,128)S(1)}, f32[656,128]{1,0:T(8,128)S(1)}, u32[]{:S(2)}, u32[]{:S(2)}) collective-permute-start(f32[656,128]{1,0:T(8,128)S(1)} %collective-permute-done.5.rest_0_), channel_id=1, source_target_pairs={{0,16},{16,0},{32,48},{48,32},{64,80},{80,64},{96,112},{112,96},{1... | collective-permute-start | bytes 1007624 | tf_op jit(solution)/shard_map/ppermute | solution.py:496
  103.7 35.5 %copy-start.3 = (s32[1,512]{1,0:T(1,128)S(1)}, s32[1,512]{1,0:T(1,128)}, u32[]{:S(2)}) copy-start(s32[1,512]{1,0:T(1,128)} %refs_15_.1) | copy-start | bytes 6148
  103.7 7.9 %collective-permute-start.7 = (f32[400,128]{1,0:T(8,128)S(1)}, f32[400,128]{1,0:T(8,128)S(1)}, u32[]{:S(2)}, u32[]{:S(2)}) collective-permute-start(f32[400,128]{1,0:T(8,128)S(1)} %get-tuple-element.44), channel_id=1, source_target_pairs={{0,2},{1,3},{2,0},{3,1},{4,6},{5,7},{6,4},{7,5},{8,10},{9,11},{10,... | collective-permute-start | bytes 614408 | tf_op jit(solution)/shard_map/ppermute | solution.py:496
  111.6 2.3 %collective-permute-start.8 = (f32[400,128]{1,0:T(8,128)S(1)}, f32[400,128]{1,0:T(8,128)S(1)}, u32[]{:S(2)}, u32[]{:S(2)}) collective-permute-start(f32[400,128]{1,0:T(8,128)S(1)} %collective-permute-done.7.rest_0_), channel_id=1, source_target_pairs={{0,16},{16,0},{32,48},{48,32},{64,80},{80,64},{96,112},{112,96},{1... | collective-permute-start | bytes 614408 | tf_op jit(solution)/shard_map/ppermute | solution.py:496
  119.3 6.4 %collective-permute-start.9 = (f32[400,128]{1,0:T(8,128)S(1)}, f32[400,128]{1,0:T(8,128)S(1)}, u32[]{:S(2)}, u32[]{:S(2)}) collective-permute-start(f32[400,128]{1,0:T(8,128)S(1)} %get-tuple-element.47), channel_id=1, source_target_pairs={{0,4},{1,5},{2,6},{3,7},{4,0},{5,1},{6,2},{7,3},{8,12},{9,13},{10,... | collective-permute-start | bytes 614408 | tf_op jit(solution)/shard_map/ppermute | solution.py:496
  130.6 4.7 %collective-permute-start.10 = (f32[136,128]{1,0:T(8,128)S(1)}, f32[136,128]{1,0:T(8,128)S(1)}, u32[]{:S(2)}, u32[]{:S(2)}) collective-permute-start(f32[136,128]{1,0:T(8,128)S(1)} %get-tuple-element.56), channel_id=1, source_target_pairs={{0,8},{1,9},{2,10},{3,11},{4,12},{5,13},{6,14},{7,15},{8,0},{9,1},... | collective-permute-start | bytes 208904 | tf_op jit(solution)/shard_map/ppermute | solution.py:496

commit v3 on v2

--- a/solution.py
+++ b/solution.py
@@ -197,7 +197,7 @@
     for level in reversed(range(levels)):
         nodes, node = (1 << levels) >> level, tree >> level
         mine, yours = (
-            [map_ref[(nodes + n - 2) * NB + i] for i in range(NB)] for n in (node, node ^ 1)
+            [map_ref[nodes + n - 2, i] for i in range(NB)] for n in (node, node ^ 1)
         )
         dropped = active(levels, level + 1)
         for child, other, base in ((mine, yours, 0), (yours, mine, 4)):
@@ -409,6 +409,7 @@
 SCALARS = pl.BlockSpec(memory_space=pltpu.SMEM)
 WHOLE = pl.BlockSpec(memory_space=pltpu.VMEM)
 PARAMS = pltpu.CompilerParams(vmem_limit_bytes=VMEM_LIMIT)
+LEAF_PARAMS = pltpu.CompilerParams(vmem_limit_bytes=62 * 1024 * 1024)
 
 
 def f32(*shape):
@@ -438,7 +439,7 @@
         in_specs=[SCALARS] + [WHOLE] * 5,
         out_specs=(WHOLE,) * 3,
         scratch_shapes=[vmem(BW, BW), vmem(BW, FW), vmem(8 * SLOTS, BW)],
-        compiler_params=PARAMS,
+        compiler_params=LEAF_PARAMS,
         name="leaf_front",
     )(plan, leaf, source, observe, zones, cells)
 
@@ -503,7 +504,7 @@
     levels = devices.bit_length() - 1
     tree = (lax.axis_index("leaf") + leaf_count * lax.axis_index("sub")).astype(jnp.int32)[None]
     core = tree & 1
-    plan = make_plan(levels, tree, block_map.reshape(-1))
+    plan = make_plan(levels, tree, block_map)
     zones = jnp.broadcast_to(log_perm[None], (devices, log_perm.shape[0]))
     all_zones = lax.all_to_all(zones, ("leaf", "sub"), 0, 0, tiled=True)
     leaf, pack, perm = leaf_front(levels, plan, leaf_matrix[0], leaf_source, observe, all_zones, zone_ids)

time: 159 us -> 161 us (1.013)
  waiting for transfers between devices: 59.5 us -> 48.4 us
  starting transfers between devices: 21.6 us -> 31.3 us
  Pallas kernels: 53.7 us -> 57.1 us
  blocking collectives: 14.8 us -> 18 us
  local copies, waits for them, and re-layouts: 6.77 us -> 4.68 us
    ppermute x11, starting transfers between devices: 10.1 us -> 19.8 us  [partner(): return lax.ppermute(block, axis, [(k, k ^ 1 << bit) for k in range(count)])]
    ppermute x11, waiting for transfers between devices: 53.5 us -> 44.4 us  [partner(): return lax.ppermute(block, axis, [(k, k ^ 1 << bit) for k in range(count)])]
    pallas_call x7, Pallas kernels: 32 us -> 36.5 us  [merge(): pl.pallas_call(functools.partial(merge_kernel, levels, level), out_shape=...]
    pallas_call x1, Pallas kernels: 16.7 us -> 13.5 us  [leaf_front(): pl.pallas_call(functools.partial(leaf_kernel, levels), out_shape=(f32(FW...]
    all_to_all x1, blocking collectives: 14.8 us -> 18 us  [shards(): shares = lax.all_to_all(partial, ('leaf', 'sub'), 0, 0, tiled=True)]
    pallas_call x1, Pallas kernels: 1.98 us -> 4.07 us  [make_plan(): pl.pallas_call(functools.partial(plan_kernel, levels), out_shape=jax.Shap...]
    all_to_all x1, waiting for transfers between devices: 6.03 us -> 4 us  [shards(): all_zones = lax.all_to_all(zones, ('leaf', 'sub'), 0, 0, tiled=True)]
  transfers between devices with their start and end apart: 12 -> 12, of which waited for: 12 -> 12; matrix products, arithmetic and copies ran while one was open for 1% -> 1% of each run, Pallas kernels for 1% -> 3%
where the time goes in v3:
time: 161 us
  Pallas kernels  57.1 us (35%)
  waiting for transfers between devices  48.4 us (30%)
  starting transfers between devices  31.3 us (19%)
  blocking collectives  18 us (11%)
  local copies, waits for them, and re-layouts  4.68 us (3%)
    ppermute x11, waiting for transfers between devices, partner(): return lax.ppermute(block, axis, [(k, k ^ 1 << bit) for k in range(count)])  44.4 us
    pallas_call x7, Pallas kernels, merge(): pl.pallas_call(functools.partial(merge_kernel, levels, level), out_shape=...  36.5 us
    ppermute x11, starting transfers between devices, partner(): return lax.ppermute(block, axis, [(k, k ^ 1 << bit) for k in range(count)])  19.8 us
    all_to_all x1, blocking collectives, shards(): shares = lax.all_to_all(partial, ('leaf', 'sub'), 0, 0, tiled=True)  18 us
    pallas_call x1, Pallas kernels, leaf_front(): pl.pallas_call(functools.partial(leaf_kernel, levels), out_shape=(f32(FW...  13.5 us
    all_to_all x1, starting transfers between devices, shards(): all_zones = lax.all_to_all(zones, ('leaf', 'sub'), 0, 0, tiled=True)  11.5 us
    pallas_call x1, Pallas kernels, make_plan(): pl.pallas_call(functools.partial(plan_kernel, levels), out_shape=jax.Shap...  4.07 us
    all_to_all x1, waiting for transfers between devices, shards(): all_zones = lax.all_to_all(zones, ('leaf', 'sub'), 0, 0, tiled=True)  4 us
  transfers between devices with their start and end apart: 12, of which 12 were waited for; matrix products, arithmetic and copies ran while one was open for 1% of the time, Pallas kernels for 3%

profile of v3, /device:TPU:1, one launch (start us, length us, event | category | flops | bytes accessed | tf_op | source)
XLA Modules:
  0.0 160.9 jit_solution(7254709598651781330)
XLA Ops:
  0.6 1.3 broadcast_in_dim.10
  2.0 11.5 %all-to-all-start = ((f32[128,1,128]{2,1,0:T(1,128)}), f32[128,1,128]{2,1,0:T(1,128)S(1)}, u32[]{:S(2)}, u32[]{:S(2)}) async-start(f32[128,1,128]{2,1,0:T(1,128)} %broadcast_in_dim.10), calls=%async_computation | async-start | bytes 131072 | tf_op jit(solution)/shard_map/all_to_all | solution.py:509
  13.5 1.5 copy.9.map_ref
  14.9 4.1 %make_plan.1.plan = s32[128]{0:T(128)} custom-call(s32[1]{0:T(128)} %bitcast.tree_ref, s32[254,4]{1,0:T(8,128)} %copy.9.map_ref), custom_call_target="tpu_custom_call" | custom-call | tf_op jit(solution)/shard_map/make_plan/pallas_call | solution.py:424
  19.0 0.0 copy-start.2
  19.0 4.0 %all-to-all-done = f32[128,1,128]{2,1,0:T(1,128)S(1)} async-done(((f32[128,1,128]{2,1,0:T(1,128)}), f32[128,1,128]{2,1,0:T(1,128)S(1)}, u32[]{:S(2)}, u32[]{:S(2)}) %all-to-all-start) | async-done | bytes 65568 | tf_op jit(solution)/shard_map/all_to_all | solution.py:509
  23.0 0.6 copy-done.5
  23.7 13.5 %leaf_front.1 = (f32[520,512]{1,0:T(8,128)}, f32[1312,128]{1,0:T(8,128)}, f32[1,512]{1,0:T(1,128)}) custom-call(s32[128]{0:T(128)} %make_plan.1.plan, f32[512,512]{1,0:T(8,128)} %bitcast.7, f32[1,512]{1,0:T(1,128)} %source.1, f32[1,512]{1,0:T(1,128)} %observe.1, f32[128,128]{1,0:T(8,128)} %bitcast.8, s32[1,512]{1,0:T(1,128)} %refs_15_.1), custom_call_target="tpu_custom_call" | custom-call | tf_op jit(solution)/shard_map/leaf_front/pallas_call | solution.py:436
  37.1 1.0 collective-permute-start
  38.1 2.0 %collective-permute-done.rest_0_ = f32[1312,128]{1,0:T(8,128)S(1)} collective-permute-done((f32[1312,128]{1,0:T(8,128)}, f32[1312,128]{1,0:T(8,128)S(1)}, u32[]{:S(2)}, u32[]{:S(2)}) %collective-permute-start) | collective-permute-done | bytes 671776 | tf_op jit(solution)/shard_map/ppermute | solution.py:497
  40.1 0.0 copy-done.2
  40.1 1.2 copy-done
  41.3 5.6 %merge_0.1 = (f32[128,512]{1,0:T(8,128)S(1)}, f32[8,128]{1,0:T(8,128)S(1)}, f32[520,512]{1,0:T(8,128)S(1)}, f32[656,128]{1,0:T(8,128)S(1)}) custom-call(s32[1]{0:T(128)S(6)} %and.5.core_ref, s32[128]{0:T(128)S(1)} %copy-done.2, f32[520,512]{1,0:T(8,128)S(1)} %copy-done, f32[1312,128]{1,0:T(8,128)S(1)} %collective-permute-done.rest_0_), custom_call_target="tpu_custom_call" | custom-call | tf_op jit(solution)/shard_map/merge_0/pallas_call | solution.py:473
  46.9 0.6 collective-permute-start.1
  47.5 8.6 %collective-permute-done.1.rest_0_ = f32[656,128]{1,0:T(8,128)S(1)} collective-permute-done((f32[656,128]{1,0:T(8,128)S(1)}, f32[656,128]{1,0:T(8,128)S(1)}, u32[]{:S(2)}, u32[]{:S(2)}) %collective-permute-start.1) | collective-permute-done | bytes 335904 | tf_op jit(solution)/shard_map/ppermute | solution.py:497
  56.0 1.2 collective-permute-start.2
  57.2 1.3 collective-permute-done.2.rest_1_
  58.5 5.7 %merge_1.1 = (f32[128,512]{1,0:T(8,128)S(1)}, f32[8,128]{1,0:T(8,128)S(1)}, f32[520,512]{1,0:T(8,128)S(1)}, f32[656,128]{1,0:T(8,128)S(1)}) custom-call(s32[1]{0:T(128)S(6)} %and.5.core_ref, s32[128]{0:T(128)S(1)} %copy-done.2, f32[520,512]{1,0:T(8,128)S(1)} %get-tuple-element.34.own, f32[656,128]{1,0:T(8,128)S(1)} %collective-permute-done.1.rest_0_, ...), custom_call_target="tpu_custom_call" | custom-call | tf_op jit(solution)/shard_map/merge_1/pallas_call | solution.py:473
  64.3 5.9 %collective-permute-start.3 = (f32[656,128]{1,0:T(8,128)S(1)}, f32[656,128]{1,0:T(8,128)S(1)}, u32[]{:S(2)}, u32[]{:S(2)}) collective-permute-start(f32[656,128]{1,0:T(8,128)S(1)} %get-tuple-element.38), channel_id=1, source_target_pairs={{0,64},{16,80},{32,96},{48,112},{64,0},{80,16},{96,32},{112,48},{1... | collective-permute-start | bytes 1007624 | tf_op jit(solution)/shard_map/ppermute | solution.py:497
  70.2 7.9 %collective-permute-done.3.rest_0_ = f32[656,128]{1,0:T(8,128)S(1)} collective-permute-done((f32[656,128]{1,0:T(8,128)S(1)}, f32[656,128]{1,0:T(8,128)S(1)}, u32[]{:S(2)}, u32[]{:S(2)}) %collective-permute-start.3) | collective-permute-done | bytes 335904 | tf_op jit(solution)/shard_map/ppermute | solution.py:497
  78.1 0.9 collective-permute-start.4
  79.0 1.3 collective-permute-done.4.rest_1_
  80.3 5.6 %merge_2.1 = (f32[128,512]{1,0:T(8,128)S(1)}, f32[8,128]{1,0:T(8,128)S(1)}, f32[520,512]{1,0:T(8,128)S(1)}, f32[656,128]{1,0:T(8,128)S(1)}) custom-call(s32[1]{0:T(128)S(6)} %and.5.core_ref, s32[128]{0:T(128)S(1)} %copy-done.2, f32[520,512]{1,0:T(8,128)S(1)} %get-tuple-element.37.own, f32[656,128]{1,0:T(8,128)S(1)} %collective-permute-done.3.rest_0_, ...), custom_call_target="tpu_custom_call" | custom-call | tf_op jit(solution)/shard_map/merge_2/pallas_call | solution.py:473
  85.8 2.3 %collective-permute-start.5 = (f32[656,128]{1,0:T(8,128)S(1)}, f32[656,128]{1,0:T(8,128)S(1)}, u32[]{:S(2)}, u32[]{:S(2)}) collective-permute-start(f32[656,128]{1,0:T(8,128)S(1)} %get-tuple-element.41), channel_id=1, source_target_pairs={{0,1},{1,0},{2,3},{3,2},{4,5},{5,4},{6,7},{7,6},{8,9},{9,8},{10,11... | collective-permute-start | bytes 1007624 | tf_op jit(solution)/shard_map/ppermute | solution.py:497
  88.1 7.9 %collective-permute-done.5.rest_0_ = f32[656,128]{1,0:T(8,128)S(1)} collective-permute-done((f32[656,128]{1,0:T(8,128)S(1)}, f32[656,128]{1,0:T(8,128)S(1)}, u32[]{:S(2)}, u32[]{:S(2)}) %collective-permute-start.5) | collective-permute-done | bytes 335904 | tf_op jit(solution)/shard_map/ppermute | solution.py:497
  96.1 0.9 collective-permute-start.6
  97.0 1.3 collective-permute-done.6.rest_1_
  98.2 5.4 %merge_3.1 = (f32[128,384]{1,0:T(8,128)S(1)}, f32[8,128]{1,0:T(8,128)S(1)}, f32[392,384]{1,0:T(8,128)S(1)}, f32[400,128]{1,0:T(8,128)S(1)}) custom-call(s32[1]{0:T(128)S(6)} %and.5.core_ref, s32[128]{0:T(128)S(1)} %copy-done.2, f32[520,512]{1,0:T(8,128)S(1)} %get-tuple-element.40.own, f32[656,128]{1,0:T(8,128)S(1)} %collective-permute-done.5.rest_0_, ...), custom_call_target="tpu_custom_call" | custom-call | tf_op jit(solution)/shard_map/merge_3/pallas_call | solution.py:473
  103.6 0.0 copy-start.1
  103.6 0.0 copy-start.3
  103.6 0.0 copy-start.4
  103.6 2.0 %collective-permute-start.7 = (f32[400,128]{1,0:T(8,128)S(1)}, f32[400,128]{1,0:T(8,128)S(1)}, u32[]{:S(2)}, u32[]{:S(2)}) collective-permute-start(f32[400,128]{1,0:T(8,128)S(1)} %get-tuple-element.44), channel_id=1, source_target_pairs={{0,2},{1,3},{2,0},{3,1},{4,6},{5,7},{6,4},{7,5},{8,10},{9,11},{10,... | collective-permute-start | bytes 614408 | tf_op jit(solution)/shard_map/ppermute | solution.py:497
  105.7 5.8 %collective-permute-done.7.rest_0_ = f32[400,128]{1,0:T(8,128)S(1)} collective-permute-done((f32[400,128]{1,0:T(8,128)S(1)}, f32[400,128]{1,0:T(8,128)S(1)}, u32[]{:S(2)}, u32[]{:S(2)}) %collective-permute-start.7) | collective-permute-done | bytes 204832 | tf_op jit(solution)/shard_map/ppermute | solution.py:497
  111.5 1.2 collective-permute-start.8
  112.7 1.1 collective-permute-done.8.rest_1_
  113.8 5.4 %merge_4.1 = (f32[128,256]{1,0:T(8,128)S(1)}, f32[8,128]{1,0:T(8,128)S(1)}, f32[264,256]{1,0:T(8,128)S(1)}, f32[400,128]{1,0:T(8,128)S(1)}) custom-call(s32[1]{0:T(128)S(6)} %and.5.core_ref, s32[128]{0:T(128)S(1)} %copy-done.2, f32[392,384]{1,0:T(8,128)S(1)} %get-tuple-element.43.own, f32[400,128]{1,0:T(8,128)S(1)} %collective-permute-done.7.rest_0_, ...), custom_call_target="tpu_custom_call" | custom-call | tf_op jit(solution)/shard_map/merge_4/pallas_call | solution.py:473
  119.2 1.2 collective-permute-start.9
  120.4 5.2 %collective-permute-done.9.rest_0_ = f32[400,128]{1,0:T(8,128)S(1)} collective-permute-done((f32[400,128]{1,0:T(8,128)S(1)}, f32[400,128]{1,0:T(8,128)S(1)}, u32[]{:S(2)}, u32[]{:S(2)}) %collective-permute-start.9) | collective-permute-done | bytes 204832 | tf_op jit(solution)/shard_map/ppermute | solution.py:497
  125.6 4.9 %merge_5.1 = (f32[128,128]{1,0:T(8,128)S(1)}, f32[8,128]{1,0:T(8,128)S(1)}, f32[136,128]{1,0:T(8,128)S(1)}, f32[136,128]{1,0:T(8,128)S(1)}) custom-call(s32[1]{0:T(128)S(6)} %and.5.core_ref, s32[128]{0:T(128)S(1)} %copy-done.2, f32[264,256]{1,0:T(8,128)S(1)} %get-tuple-element.46.own, f32[400,128]{1,0:T(8,128)S(1)} %collective-permute-done.9.rest_0_), custom_call_target="tpu_custom_call" | custom-call | tf_op jit(solution)/shard_map/merge_5/pallas_call | solution.py:473
  130.5 2.7 %collective-permute-start.10 = (f32[136,128]{1,0:T(8,128)S(1)}, f32[136,128]{1,0:T(8,128)S(1)}, u32[]{:S(2)}, u32[]{:S(2)}) collective-permute-start(f32[136,128]{1,0:T(8,128)S(1)} %get-tuple-element.56), channel_id=1, source_target_pairs={{0,8},{1,9},{2,10},{3,11},{4,12},{5,13},{6,14},{7,15},{8,0},{9,1},... | collective-permute-start | bytes 208904 | tf_op jit(solution)/shard_map/ppermute | solution.py:497
  133.2 2.1 %collective-permute-done.10.rest_0_ = f32[136,128]{1,0:T(8,128)S(1)} collective-permute-done((f32[136,128]{1,0:T(8,128)S(1)}, f32[136,128]{1,0:T(8,128)S(1)}, u32[]{:S(2)}, u32[]{:S(2)}) %collective-permute-start.10) | collective-permute-done | bytes 69664 | tf_op jit(solution)/shard_map/ppermute | solution.py:497
  135.2 3.9 %merge_6.1.refs_12_ = f32[8,128]{1,0:T(8,128)S(1)} custom-call(s32[1]{0:T(128)S(6)} %and.5.core_ref, s32[128]{0:T(128)S(1)} %copy-done.2, f32[136,128]{1,0:T(8,128)S(1)} %get-tuple-element.55.own, f32[136,128]{1,0:T(8,128)S(1)} %collective-permute-done.10.rest_0_), custom_call_target="tpu_custom_call" | custom-call | tf_op jit(solution)/shard_map/merge_6/pallas_call | solution.py:473
  139.2 0.0 copy-done.1
  139.2 0.0 copy-done.3
  139.2 0.0 copy-done.4
  139.2 3.1 %recover.1 = (f32[1,512]{1,0:T(1,128)}, f32[128,128]{1,0:T(8,128)S(1)}) custom-call(s32[128]{0:T(128)S(1)} %copy-done.2, f32[128,512]{1,0:T(8,128)S(1)} %get-tuple-element.33.refs_0_, f32[128,512]{1,0:T(8,128)S(1)} %get-tuple-element.36.refs_1_, f32[128,512]{1,0:T(8,128)S(1)} %get-tuple-element.39.refs_2_, f32[128,384]{1,0:T(8,128)S(1)} %get-tuple-element.42.refs_3_, ...), custom_call_target="tpu_custom_call" | custom-call | tf_op jit(solution)/shard_map/recover/pallas_call | solution.py:485
  142.3 18.0 %all_to_all.17 = f32[128,1,128]{2,1,0:T(1,128)S(1)} all-to-all(f32[128,1,128]{2,1,0:T(1,128)S(1)} %bitcast.6), channel_id=1, replica_groups=mesh['leaf'=8,'sub'=16] {'leaf','sub'}, dimensions={0} | all-to-all | bytes 131072 | tf_op jit(solution)/shard_map/all_to_all | solution.py:530
  160.3 0.7 reduce_sum.9
  (2 shorter events, 0.0 us)
Async XLA Ops:
  2.0 21.1 %all-to-all-start = ((f32[128,1,128]{2,1,0:T(1,128)}), f32[128,1,128]{2,1,0:T(1,128)S(1)}, u32[]{:S(2)}, u32[]{:S(2)}) async-start(f32[128,1,128]{2,1,0:T(1,128)} %broadcast_in_dim.10), calls=%async_computation | async-start | bytes 131072 | tf_op jit(solution)/shard_map/all_to_all | solution.py:509
  19.0 21.1 %copy-start.2 = (s32[128]{0:T(128)S(1)}, s32[128]{0:T(128)}, u32[]{:S(2)}) copy-start(s32[128]{0:T(128)} %make_plan.1.plan) | copy-start | bytes 1540
  23.0 0.6 copy-start.5
  37.1 2.9 %collective-permute-start = (f32[1312,128]{1,0:T(8,128)}, f32[1312,128]{1,0:T(8,128)S(1)}, u32[]{:S(2)}, u32[]{:S(2)}) collective-permute-start(f32[1312,128]{1,0:T(8,128)} %get-tuple-element.32), channel_id=1, source_target_pairs={{0,16},{16,0},{32,48},{48,32},{64,80},{80,64},{96,112},{112,96},{1... | collective-permute-start | bytes 2015240 | tf_op jit(solution)/shard_map/ppermute | solution.py:497
  40.1 1.2 copy-start
  46.9 9.2 %collective-permute-start.1 = (f32[656,128]{1,0:T(8,128)S(1)}, f32[656,128]{1,0:T(8,128)S(1)}, u32[]{:S(2)}, u32[]{:S(2)}) collective-permute-start(f32[656,128]{1,0:T(8,128)S(1)} %get-tuple-element.35), channel_id=1, source_target_pairs={{0,32},{16,48},{32,0},{48,16},{64,96},{80,112},{96,64},{112,80},{1... | collective-permute-start | bytes 1007624 | tf_op jit(solution)/shard_map/ppermute | solution.py:497
  56.0 2.5 %collective-permute-start.2 = (f32[656,128]{1,0:T(8,128)S(1)}, f32[656,128]{1,0:T(8,128)S(1)}, u32[]{:S(2)}, u32[]{:S(2)}) collective-permute-start(f32[656,128]{1,0:T(8,128)S(1)} %collective-permute-done.1.rest_0_), channel_id=1, source_target_pairs={{0,16},{16,0},{32,48},{48,32},{64,80},{80,64},{96,112},{112,96},{1... | collective-permute-start | bytes 1007624 | tf_op jit(solution)/shard_map/ppermute | solution.py:497
  64.3 13.9 %collective-permute-start.3 = (f32[656,128]{1,0:T(8,128)S(1)}, f32[656,128]{1,0:T(8,128)S(1)}, u32[]{:S(2)}, u32[]{:S(2)}) collective-permute-start(f32[656,128]{1,0:T(8,128)S(1)} %get-tuple-element.38), channel_id=1, source_target_pairs={{0,64},{16,80},{32,96},{48,112},{64,0},{80,16},{96,32},{112,48},{1... | collective-permute-start | bytes 1007624 | tf_op jit(solution)/shard_map/ppermute | solution.py:497
  78.1 2.2 %collective-permute-start.4 = (f32[656,128]{1,0:T(8,128)S(1)}, f32[656,128]{1,0:T(8,128)S(1)}, u32[]{:S(2)}, u32[]{:S(2)}) collective-permute-start(f32[656,128]{1,0:T(8,128)S(1)} %collective-permute-done.3.rest_0_), channel_id=1, source_target_pairs={{0,16},{16,0},{32,48},{48,32},{64,80},{80,64},{96,112},{112,96},{1... | collective-permute-start | bytes 1007624 | tf_op jit(solution)/shard_map/ppermute | solution.py:497
  85.8 10.2 %collective-permute-start.5 = (f32[656,128]{1,0:T(8,128)S(1)}, f32[656,128]{1,0:T(8,128)S(1)}, u32[]{:S(2)}, u32[]{:S(2)}) collective-permute-start(f32[656,128]{1,0:T(8,128)S(1)} %get-tuple-element.41), channel_id=1, source_target_pairs={{0,1},{1,0},{2,3},{3,2},{4,5},{5,4},{6,7},{7,6},{8,9},{9,8},{10,11... | collective-permute-start | bytes 1007624 | tf_op jit(solution)/shard_map/ppermute | solution.py:497
  96.1 2.2 %collective-permute-start.6 = (f32[656,128]{1,0:T(8,128)S(1)}, f32[656,128]{1,0:T(8,128)S(1)}, u32[]{:S(2)}, u32[]{:S(2)}) collective-permute-start(f32[656,128]{1,0:T(8,128)S(1)} %collective-permute-done.5.rest_0_), channel_id=1, source_target_pairs={{0,16},{16,0},{32,48},{48,32},{64,80},{80,64},{96,112},{112,96},{1... | collective-permute-start | bytes 1007624 | tf_op jit(solution)/shard_map/ppermute | solution.py:497
  103.6 35.6 %copy-start.1 = (f32[520,512]{1,0:T(8,128)S(1)}, f32[520,512]{1,0:T(8,128)}, u32[]{:S(2)}) copy-start(f32[520,512]{1,0:T(8,128)} %get-tuple-element.31.own.refs_13_) | copy-start | bytes 3194884
  103.6 35.5 %copy-start.3 = (s32[1,512]{1,0:T(1,128)S(1)}, s32[1,512]{1,0:T(1,128)}, u32[]{:S(2)}) copy-start(s32[1,512]{1,0:T(1,128)} %refs_15_.1) | copy-start | bytes 6148
  103.6 35.5 %copy-start.4 = (f32[1,512]{1,0:T(1,128)S(1)}, f32[1,512]{1,0:T(1,128)}, u32[]{:S(2)}) copy-start(f32[1,512]{1,0:T(1,128)} %get-tuple-element.57.refs_14_) | copy-start | bytes 6148
  103.6 7.9 %collective-permute-start.7 = (f32[400,128]{1,0:T(8,128)S(1)}, f32[400,128]{1,0:T(8,128)S(1)}, u32[]{:S(2)}, u32[]{:S(2)}) collective-permute-start(f32[400,128]{1,0:T(8,128)S(1)} %get-tuple-element.44), channel_id=1, source_target_pairs={{0,2},{1,3},{2,0},{3,1},{4,6},{5,7},{6,4},{7,5},{8,10},{9,11},{10,... | collective-permute-start | bytes 614408 | tf_op jit(solution)/shard_map/ppermute | solution.py:497
  111.5 2.3 %collective-permute-start.8 = (f32[400,128]{1,0:T(8,128)S(1)}, f32[400,128]{1,0:T(8,128)S(1)}, u32[]{:S(2)}, u32[]{:S(2)}) collective-permute-start(f32[400,128]{1,0:T(8,128)S(1)} %collective-permute-done.7.rest_0_), channel_id=1, source_target_pairs={{0,16},{16,0},{32,48},{48,32},{64,80},{80,64},{96,112},{112,96},{1... | collective-permute-start | bytes 614408 | tf_op jit(solution)/shard_map/ppermute | solution.py:497
  119.2 6.4 %collective-permute-start.9 = (f32[400,128]{1,0:T(8,128)S(1)}, f32[400,128]{1,0:T(8,128)S(1)}, u32[]{:S(2)}, u32[]{:S(2)}) collective-permute-start(f32[400,128]{1,0:T(8,128)S(1)} %get-tuple-element.47), channel_id=1, source_target_pairs={{0,4},{1,5},{2,6},{3,7},{4,0},{5,1},{6,2},{7,3},{8,12},{9,13},{10,... | collective-permute-start | bytes 614408 | tf_op jit(solution)/shard_map/ppermute | solution.py:497
  130.5 4.7 %collective-permute-start.10 = (f32[136,128]{1,0:T(8,128)S(1)}, f32[136,128]{1,0:T(8,128)S(1)}, u32[]{:S(2)}, u32[]{:S(2)}) collective-permute-start(f32[136,128]{1,0:T(8,128)S(1)} %get-tuple-element.56), channel_id=1, source_target_pairs={{0,8},{1,9},{2,10},{3,11},{4,12},{5,13},{6,14},{7,15},{8,0},{9,1},... | collective-permute-start | bytes 208904 | tf_op jit(solution)/shard_map/ppermute | solution.py:497

commit v4 on v2

--- a/solution.py
+++ b/solution.py
@@ -409,6 +409,7 @@
 SCALARS = pl.BlockSpec(memory_space=pltpu.SMEM)
 WHOLE = pl.BlockSpec(memory_space=pltpu.VMEM)
 PARAMS = pltpu.CompilerParams(vmem_limit_bytes=VMEM_LIMIT)
+LEAF_PARAMS = pltpu.CompilerParams(vmem_limit_bytes=62 * 1024 * 1024)
 
 
 def f32(*shape):
@@ -438,7 +439,7 @@
         in_specs=[SCALARS] + [WHOLE] * 5,
         out_specs=(WHOLE,) * 3,
         scratch_shapes=[vmem(BW, BW), vmem(BW, FW), vmem(8 * SLOTS, BW)],
-        compiler_params=PARAMS,
+        compiler_params=LEAF_PARAMS,
         name="leaf_front",
     )(plan, leaf, source, observe, zones, cells)
 

time: 159 us -> 159 us (level)
  starting transfers between devices: 21.6 us -> 40.1 us
  Pallas kernels: 53.7 us -> 41.1 us
  waiting for transfers between devices: 59.5 us -> 51.7 us
  blocking collectives: 14.8 us -> 19.8 us
  local copies, waits for them, and re-layouts: 6.77 us -> 4.73 us
    ppermute x11, starting transfers between devices: 10.1 us -> 28.6 us  [partner(): return lax.ppermute(block, axis, [(k, k ^ 1 << bit) for k in range(count)])]
    pallas_call x1, Pallas kernels: 16.7 us -> 8.27 us  [leaf_front(): pl.pallas_call(functools.partial(leaf_kernel, levels), out_shape=(f32(FW...]
    ppermute x11, waiting for transfers between devices: 53.5 us -> 45.7 us  [partner(): return lax.ppermute(block, axis, [(k, k ^ 1 << bit) for k in range(count)])]
    all_to_all x1, blocking collectives: 14.8 us -> 19.8 us  [shards(): shares = lax.all_to_all(partial, ('leaf', 'sub'), 0, 0, tiled=True)]
    pallas_call x7, Pallas kernels: 32 us -> 27.8 us  [merge(): pl.pallas_call(functools.partial(merge_kernel, levels, level), out_shape=...]
    unnamed x13, local copies, waits for them, and re-layouts: 4.74 us -> 2.7 us
where the time goes in v4:
time: 159 us
  waiting for transfers between devices  51.7 us (33%)
  Pallas kernels  41.1 us (26%)
  starting transfers between devices  40.1 us (25%)
  blocking collectives  19.8 us (12%)
  local copies, waits for them, and re-layouts  4.73 us (3%)
    ppermute x11, waiting for transfers between devices, partner(): return lax.ppermute(block, axis, [(k, k ^ 1 << bit) for k in range(count)])  45.7 us
    ppermute x11, starting transfers between devices, partner(): return lax.ppermute(block, axis, [(k, k ^ 1 << bit) for k in range(count)])  28.6 us
    pallas_call x7, Pallas kernels, merge(): pl.pallas_call(functools.partial(merge_kernel, levels, level), out_shape=...  27.8 us
    all_to_all x1, blocking collectives, shards(): shares = lax.all_to_all(partial, ('leaf', 'sub'), 0, 0, tiled=True)  19.8 us
    all_to_all x1, starting transfers between devices, shards(): all_zones = lax.all_to_all(zones, ('leaf', 'sub'), 0, 0, tiled=True)  11.5 us
    pallas_call x1, Pallas kernels, leaf_front(): pl.pallas_call(functools.partial(leaf_kernel, levels), out_shape=(f32(FW...  8.27 us
    all_to_all x1, waiting for transfers between devices, shards(): all_zones = lax.all_to_all(zones, ('leaf', 'sub'), 0, 0, tiled=True)  6.02 us
  transfers between devices with their start and end apart: 12, of which 12 were waited for; matrix products, arithmetic and copies ran while one was open for 1% of the time, Pallas kernels for 1%

profile of v4, /device:TPU:1, one launch (start us, length us, event | category | flops | bytes accessed | tf_op | source)
XLA Modules:
  0.0 158.9 jit_solution(13200736270124335045)
XLA Ops:
  0.6 1.3 broadcast_in_dim.10
  1.9 11.5 %all-to-all-start = ((f32[128,1,128]{2,1,0:T(1,128)}), f32[128,1,128]{2,1,0:T(1,128)S(1)}, u32[]{:S(2)}, u32[]{:S(2)}) async-start(f32[128,1,128]{2,1,0:T(1,128)} %broadcast_in_dim.10), calls=%async_computation | async-start | bytes 131072 | tf_op jit(solution)/shard_map/all_to_all | solution.py:509
  13.5 0.8 copy.9
  14.3 0.7 reshape.15.map_ref
  15.0 2.0 %make_plan.1.plan = s32[128]{0:T(128)} custom-call(s32[1]{0:T(128)} %bitcast.tree_ref, s32[1016]{0:T(1024)} %reshape.15.map_ref), custom_call_target="tpu_custom_call" | custom-call | tf_op jit(solution)/shard_map/make_plan/pallas_call | solution.py:424
  17.0 0.0 copy-start.2
  17.0 6.0 %all-to-all-done = f32[128,1,128]{2,1,0:T(1,128)S(1)} async-done(((f32[128,1,128]{2,1,0:T(1,128)}), f32[128,1,128]{2,1,0:T(1,128)S(1)}, u32[]{:S(2)}, u32[]{:S(2)}) %all-to-all-start) | async-done | bytes 65568 | tf_op jit(solution)/shard_map/all_to_all | solution.py:509
  23.0 0.6 copy-done.5
  23.6 8.3 %leaf_front.1 = (f32[520,512]{1,0:T(8,128)}, f32[1312,128]{1,0:T(8,128)}, f32[1,512]{1,0:T(1,128)}) custom-call(s32[128]{0:T(128)} %make_plan.1.plan, f32[512,512]{1,0:T(8,128)} %bitcast.7, f32[1,512]{1,0:T(1,128)} %source.1, f32[1,512]{1,0:T(1,128)} %observe.1, f32[128,128]{1,0:T(8,128)} %bitcast.8, s32[1,512]{1,0:T(1,128)} %refs_15_.1), custom_call_target="tpu_custom_call" | custom-call | tf_op jit(solution)/shard_map/leaf_front/pallas_call | solution.py:436
  31.9 1.0 collective-permute-start
  32.9 2.0 %collective-permute-done.rest_0_ = f32[1312,128]{1,0:T(8,128)S(1)} collective-permute-done((f32[1312,128]{1,0:T(8,128)}, f32[1312,128]{1,0:T(8,128)S(1)}, u32[]{:S(2)}, u32[]{:S(2)}) %collective-permute-start) | collective-permute-done | bytes 671776 | tf_op jit(solution)/shard_map/ppermute | solution.py:497
  34.9 0.0 copy-done.2
  34.9 1.2 copy-done
  36.1 5.7 %merge_0.1 = (f32[128,512]{1,0:T(8,128)S(1)}, f32[8,128]{1,0:T(8,128)S(1)}, f32[520,512]{1,0:T(8,128)S(1)}, f32[656,128]{1,0:T(8,128)S(1)}) custom-call(s32[1]{0:T(128)S(6)} %and.5.core_ref, s32[128]{0:T(128)S(1)} %copy-done.2, f32[520,512]{1,0:T(8,128)S(1)} %copy-done, f32[1312,128]{1,0:T(8,128)S(1)} %collective-permute-done.rest_0_), custom_call_target="tpu_custom_call" | custom-call | tf_op jit(solution)/shard_map/merge_0/pallas_call | solution.py:473
  41.8 6.2 %collective-permute-start.1 = (f32[656,128]{1,0:T(8,128)S(1)}, f32[656,128]{1,0:T(8,128)S(1)}, u32[]{:S(2)}, u32[]{:S(2)}) collective-permute-start(f32[656,128]{1,0:T(8,128)S(1)} %get-tuple-element.35), channel_id=1, source_target_pairs={{0,32},{16,48},{32,0},{48,16},{64,96},{80,112},{96,64},{112,80},{1... | collective-permute-start | bytes 1007624 | tf_op jit(solution)/shard_map/ppermute | solution.py:497
  48.0 8.0 %collective-permute-done.1.rest_0_ = f32[656,128]{1,0:T(8,128)S(1)} collective-permute-done((f32[656,128]{1,0:T(8,128)S(1)}, f32[656,128]{1,0:T(8,128)S(1)}, u32[]{:S(2)}, u32[]{:S(2)}) %collective-permute-start.1) | collective-permute-done | bytes 335904 | tf_op jit(solution)/shard_map/ppermute | solution.py:497
  55.9 0.9 collective-permute-start.2
  56.8 1.3 collective-permute-done.2.rest_1_
  58.1 1.1 merge_1.1
  59.2 11.0 %collective-permute-start.3 = (f32[656,128]{1,0:T(8,128)S(1)}, f32[656,128]{1,0:T(8,128)S(1)}, u32[]{:S(2)}, u32[]{:S(2)}) collective-permute-start(f32[656,128]{1,0:T(8,128)S(1)} %get-tuple-element.38), channel_id=1, source_target_pairs={{0,64},{16,80},{32,96},{48,112},{64,0},{80,16},{96,32},{112,48},{1... | collective-permute-start | bytes 1007624 | tf_op jit(solution)/shard_map/ppermute | solution.py:497
  70.2 7.9 %collective-permute-done.3.rest_0_ = f32[656,128]{1,0:T(8,128)S(1)} collective-permute-done((f32[656,128]{1,0:T(8,128)S(1)}, f32[656,128]{1,0:T(8,128)S(1)}, u32[]{:S(2)}, u32[]{:S(2)}) %collective-permute-start.3) | collective-permute-done | bytes 335904 | tf_op jit(solution)/shard_map/ppermute | solution.py:497
  78.2 0.9 collective-permute-start.4
  79.0 1.3 collective-permute-done.4.rest_1_
  80.3 5.6 %merge_2.1 = (f32[128,512]{1,0:T(8,128)S(1)}, f32[8,128]{1,0:T(8,128)S(1)}, f32[520,512]{1,0:T(8,128)S(1)}, f32[656,128]{1,0:T(8,128)S(1)}) custom-call(s32[1]{0:T(128)S(6)} %and.5.core_ref, s32[128]{0:T(128)S(1)} %copy-done.2, f32[520,512]{1,0:T(8,128)S(1)} %get-tuple-element.37.own, f32[656,128]{1,0:T(8,128)S(1)} %collective-permute-done.3.rest_0_, ...), custom_call_target="tpu_custom_call" | custom-call | tf_op jit(solution)/shard_map/merge_2/pallas_call | solution.py:473
  85.9 2.6 %collective-permute-start.5 = (f32[656,128]{1,0:T(8,128)S(1)}, f32[656,128]{1,0:T(8,128)S(1)}, u32[]{:S(2)}, u32[]{:S(2)}) collective-permute-start(f32[656,128]{1,0:T(8,128)S(1)} %get-tuple-element.41), channel_id=1, source_target_pairs={{0,1},{1,0},{2,3},{3,2},{4,5},{5,4},{6,7},{7,6},{8,9},{9,8},{10,11... | collective-permute-start | bytes 1007624 | tf_op jit(solution)/shard_map/ppermute | solution.py:497
  88.6 7.9 %collective-permute-done.5.rest_0_ = f32[656,128]{1,0:T(8,128)S(1)} collective-permute-done((f32[656,128]{1,0:T(8,128)S(1)}, f32[656,128]{1,0:T(8,128)S(1)}, u32[]{:S(2)}, u32[]{:S(2)}) %collective-permute-start.5) | collective-permute-done | bytes 335904 | tf_op jit(solution)/shard_map/ppermute | solution.py:497
  96.5 0.9 collective-permute-start.6
  97.4 1.3 collective-permute-done.6.rest_1_
  98.7 5.4 %merge_3.1 = (f32[128,384]{1,0:T(8,128)S(1)}, f32[8,128]{1,0:T(8,128)S(1)}, f32[392,384]{1,0:T(8,128)S(1)}, f32[400,128]{1,0:T(8,128)S(1)}) custom-call(s32[1]{0:T(128)S(6)} %and.5.core_ref, s32[128]{0:T(128)S(1)} %copy-done.2, f32[520,512]{1,0:T(8,128)S(1)} %get-tuple-element.40.own, f32[656,128]{1,0:T(8,128)S(1)} %collective-permute-done.5.rest_0_, ...), custom_call_target="tpu_custom_call" | custom-call | tf_op jit(solution)/shard_map/merge_3/pallas_call | solution.py:473
  104.1 0.0 copy-start.1
  104.1 0.0 copy-start.3
  104.1 0.0 copy-start.4
  104.1 1.6 collective-permute-start.7
  105.7 6.3 %collective-permute-done.7.rest_0_ = f32[400,128]{1,0:T(8,128)S(1)} collective-permute-done((f32[400,128]{1,0:T(8,128)S(1)}, f32[400,128]{1,0:T(8,128)S(1)}, u32[]{:S(2)}, u32[]{:S(2)}) %collective-permute-start.7) | collective-permute-done | bytes 204832 | tf_op jit(solution)/shard_map/ppermute | solution.py:497
  112.0 1.2 collective-permute-start.8
  113.2 1.1 collective-permute-done.8.rest_1_
  114.3 5.4 %merge_4.1 = (f32[128,256]{1,0:T(8,128)S(1)}, f32[8,128]{1,0:T(8,128)S(1)}, f32[264,256]{1,0:T(8,128)S(1)}, f32[400,128]{1,0:T(8,128)S(1)}) custom-call(s32[1]{0:T(128)S(6)} %and.5.core_ref, s32[128]{0:T(128)S(1)} %copy-done.2, f32[392,384]{1,0:T(8,128)S(1)} %get-tuple-element.43.own, f32[400,128]{1,0:T(8,128)S(1)} %collective-permute-done.7.rest_0_, ...), custom_call_target="tpu_custom_call" | custom-call | tf_op jit(solution)/shard_map/merge_4/pallas_call | solution.py:473
  119.7 1.5 collective-permute-start.9
  121.2 4.9 %collective-permute-done.9.rest_0_ = f32[400,128]{1,0:T(8,128)S(1)} collective-permute-done((f32[400,128]{1,0:T(8,128)S(1)}, f32[400,128]{1,0:T(8,128)S(1)}, u32[]{:S(2)}, u32[]{:S(2)}) %collective-permute-start.9) | collective-permute-done | bytes 204832 | tf_op jit(solution)/shard_map/ppermute | solution.py:497
  126.1 0.6 merge_5.1
  126.7 0.9 collective-permute-start.10
  127.6 3.8 %collective-permute-done.10.rest_0_ = f32[136,128]{1,0:T(8,128)S(1)} collective-permute-done((f32[136,128]{1,0:T(8,128)S(1)}, f32[136,128]{1,0:T(8,128)S(1)}, u32[]{:S(2)}, u32[]{:S(2)}) %collective-permute-start.10) | collective-permute-done | bytes 69664 | tf_op jit(solution)/shard_map/ppermute | solution.py:497
  131.4 3.9 %merge_6.1.refs_12_ = f32[8,128]{1,0:T(8,128)S(1)} custom-call(s32[1]{0:T(128)S(6)} %and.5.core_ref, s32[128]{0:T(128)S(1)} %copy-done.2, f32[136,128]{1,0:T(8,128)S(1)} %get-tuple-element.55.own, f32[136,128]{1,0:T(8,128)S(1)} %collective-permute-done.10.rest_0_), custom_call_target="tpu_custom_call" | custom-call | tf_op jit(solution)/shard_map/merge_6/pallas_call | solution.py:473
  135.3 0.0 copy-done.3
  135.4 0.0 copy-done.4
  135.4 3.1 %recover.1 = (f32[1,512]{1,0:T(1,128)}, f32[128,128]{1,0:T(8,128)S(1)}) custom-call(s32[128]{0:T(128)S(1)} %copy-done.2, f32[128,512]{1,0:T(8,128)S(1)} %get-tuple-element.33.refs_0_, f32[128,512]{1,0:T(8,128)S(1)} %get-tuple-element.36.refs_1_, f32[128,512]{1,0:T(8,128)S(1)} %get-tuple-element.39.refs_2_, f32[128,384]{1,0:T(8,128)S(1)} %get-tuple-element.42.refs_3_, ...), custom_call_target="tpu_custom_call" | custom-call | tf_op jit(solution)/shard_map/recover/pallas_call | solution.py:485
  138.5 19.8 %all_to_all.17 = f32[128,1,128]{2,1,0:T(1,128)S(1)} all-to-all(f32[128,1,128]{2,1,0:T(1,128)S(1)} %bitcast.6), channel_id=1, replica_groups=mesh['leaf'=8,'sub'=16] {'leaf','sub'}, dimensions={0} | all-to-all | bytes 131072 | tf_op jit(solution)/shard_map/all_to_all | solution.py:530
  158.2 0.7 reduce_sum.9
  (3 shorter events, 0.0 us)
Async XLA Ops:
  1.9 21.1 %all-to-all-start = ((f32[128,1,128]{2,1,0:T(1,128)}), f32[128,1,128]{2,1,0:T(1,128)S(1)}, u32[]{:S(2)}, u32[]{:S(2)}) async-start(f32[128,1,128]{2,1,0:T(1,128)} %broadcast_in_dim.10), calls=%async_computation | async-start | bytes 131072 | tf_op jit(solution)/shard_map/all_to_all | solution.py:509
  17.0 17.9 %copy-start.2 = (s32[128]{0:T(128)S(1)}, s32[128]{0:T(128)}, u32[]{:S(2)}) copy-start(s32[128]{0:T(128)} %make_plan.1.plan) | copy-start | bytes 1540
  23.0 0.6 copy-start.5
  31.9 2.9 %collective-permute-start = (f32[1312,128]{1,0:T(8,128)}, f32[1312,128]{1,0:T(8,128)S(1)}, u32[]{:S(2)}, u32[]{:S(2)}) collective-permute-start(f32[1312,128]{1,0:T(8,128)} %get-tuple-element.32), channel_id=1, source_target_pairs={{0,16},{16,0},{32,48},{48,32},{64,80},{80,64},{96,112},{112,96},{1... | collective-permute-start | bytes 2015240 | tf_op jit(solution)/shard_map/ppermute | solution.py:497
  34.9 1.2 copy-start
  41.8 14.1 %collective-permute-start.1 = (f32[656,128]{1,0:T(8,128)S(1)}, f32[656,128]{1,0:T(8,128)S(1)}, u32[]{:S(2)}, u32[]{:S(2)}) collective-permute-start(f32[656,128]{1,0:T(8,128)S(1)} %get-tuple-element.35), channel_id=1, source_target_pairs={{0,32},{16,48},{32,0},{48,16},{64,96},{80,112},{96,64},{112,80},{1... | collective-permute-start | bytes 1007624 | tf_op jit(solution)/shard_map/ppermute | solution.py:497
  55.9 2.2 %collective-permute-start.2 = (f32[656,128]{1,0:T(8,128)S(1)}, f32[656,128]{1,0:T(8,128)S(1)}, u32[]{:S(2)}, u32[]{:S(2)}) collective-permute-start(f32[656,128]{1,0:T(8,128)S(1)} %collective-permute-done.1.rest_0_), channel_id=1, source_target_pairs={{0,16},{16,0},{32,48},{48,32},{64,80},{80,64},{96,112},{112,96},{1... | collective-permute-start | bytes 1007624 | tf_op jit(solution)/shard_map/ppermute | solution.py:497
  59.2 18.9 %collective-permute-start.3 = (f32[656,128]{1,0:T(8,128)S(1)}, f32[656,128]{1,0:T(8,128)S(1)}, u32[]{:S(2)}, u32[]{:S(2)}) collective-permute-start(f32[656,128]{1,0:T(8,128)S(1)} %get-tuple-element.38), channel_id=1, source_target_pairs={{0,64},{16,80},{32,96},{48,112},{64,0},{80,16},{96,32},{112,48},{1... | collective-permute-start | bytes 1007624 | tf_op jit(solution)/shard_map/ppermute | solution.py:497
  78.2 2.2 %collective-permute-start.4 = (f32[656,128]{1,0:T(8,128)S(1)}, f32[656,128]{1,0:T(8,128)S(1)}, u32[]{:S(2)}, u32[]{:S(2)}) collective-permute-start(f32[656,128]{1,0:T(8,128)S(1)} %collective-permute-done.3.rest_0_), channel_id=1, source_target_pairs={{0,16},{16,0},{32,48},{48,32},{64,80},{80,64},{96,112},{112,96},{1... | collective-permute-start | bytes 1007624 | tf_op jit(solution)/shard_map/ppermute | solution.py:497
  85.9 10.6 %collective-permute-start.5 = (f32[656,128]{1,0:T(8,128)S(1)}, f32[656,128]{1,0:T(8,128)S(1)}, u32[]{:S(2)}, u32[]{:S(2)}) collective-permute-start(f32[656,128]{1,0:T(8,128)S(1)} %get-tuple-element.41), channel_id=1, source_target_pairs={{0,1},{1,0},{2,3},{3,2},{4,5},{5,4},{6,7},{7,6},{8,9},{9,8},{10,11... | collective-permute-start | bytes 1007624 | tf_op jit(solution)/shard_map/ppermute | solution.py:497
  96.5 2.2 %collective-permute-start.6 = (f32[656,128]{1,0:T(8,128)S(1)}, f32[656,128]{1,0:T(8,128)S(1)}, u32[]{:S(2)}, u32[]{:S(2)}) collective-permute-start(f32[656,128]{1,0:T(8,128)S(1)} %collective-permute-done.5.rest_0_), channel_id=1, source_target_pairs={{0,16},{16,0},{32,48},{48,32},{64,80},{80,64},{96,112},{112,96},{1... | collective-permute-start | bytes 1007624 | tf_op jit(solution)/shard_map/ppermute | solution.py:497
  104.1 31.2 %copy-start.1 = (f32[520,512]{1,0:T(8,128)S(1)}, f32[520,512]{1,0:T(8,128)}, u32[]{:S(2)}) copy-start(f32[520,512]{1,0:T(8,128)} %get-tuple-element.31.own.refs_13_) | copy-start | bytes 3194884
  104.1 31.2 %copy-start.3 = (s32[1,512]{1,0:T(1,128)S(1)}, s32[1,512]{1,0:T(1,128)}, u32[]{:S(2)}) copy-start(s32[1,512]{1,0:T(1,128)} %refs_15_.1) | copy-start | bytes 6148
  104.1 31.2 %copy-start.4 = (f32[1,512]{1,0:T(1,128)S(1)}, f32[1,512]{1,0:T(1,128)}, u32[]{:S(2)}) copy-start(f32[1,512]{1,0:T(1,128)} %get-tuple-element.57.refs_14_) | copy-start | bytes 6148
  104.1 7.9 %collective-permute-start.7 = (f32[400,128]{1,0:T(8,128)S(1)}, f32[400,128]{1,0:T(8,128)S(1)}, u32[]{:S(2)}, u32[]{:S(2)}) collective-permute-start(f32[400,128]{1,0:T(8,128)S(1)} %get-tuple-element.44), channel_id=1, source_target_pairs={{0,2},{1,3},{2,0},{3,1},{4,6},{5,7},{6,4},{7,5},{8,10},{9,11},{10,... | collective-permute-start | bytes 614408 | tf_op jit(solution)/shard_map/ppermute | solution.py:497
  112.0 2.3 %collective-permute-start.8 = (f32[400,128]{1,0:T(8,128)S(1)}, f32[400,128]{1,0:T(8,128)S(1)}, u32[]{:S(2)}, u32[]{:S(2)}) collective-permute-start(f32[400,128]{1,0:T(8,128)S(1)} %collective-permute-done.7.rest_0_), channel_id=1, source_target_pairs={{0,16},{16,0},{32,48},{48,32},{64,80},{80,64},{96,112},{112,96},{1... | collective-permute-start | bytes 614408 | tf_op jit(solution)/shard_map/ppermute | solution.py:497
  119.7 6.4 %collective-permute-start.9 = (f32[400,128]{1,0:T(8,128)S(1)}, f32[400,128]{1,0:T(8,128)S(1)}, u32[]{:S(2)}, u32[]{:S(2)}) collective-permute-start(f32[400,128]{1,0:T(8,128)S(1)} %get-tuple-element.47), channel_id=1, source_target_pairs={{0,4},{1,5},{2,6},{3,7},{4,0},{5,1},{6,2},{7,3},{8,12},{9,13},{10,... | collective-permute-start | bytes 614408 | tf_op jit(solution)/shard_map/ppermute | solution.py:497
  126.7 4.7 %collective-permute-start.10 = (f32[136,128]{1,0:T(8,128)S(1)}, f32[136,128]{1,0:T(8,128)S(1)}, u32[]{:S(2)}, u32[]{:S(2)}) collective-permute-start(f32[136,128]{1,0:T(8,128)S(1)} %get-tuple-element.56), channel_id=1, source_target_pairs={{0,8},{1,9},{2,10},{3,11},{4,12},{5,13},{6,14},{7,15},{8,0},{9,1},... | collective-permute-start | bytes 208904 | tf_op jit(solution)/shard_map/ppermute | solution.py:497
